TPU v7x, 128 devices: a whole 4x4x4 slice. The times are simulated.
128 devices in a mesh: pipe: 2 (over y_hi), dp: 32 (over x, y_lo, z), tensor: 2 (over core).
Axes of the slice: x: 4, y: 4 (y_hi: 2, y_lo: 2; y = y_hi * 2 + y_lo), z: 4, core: 2. Of those that a mesh axis runs over, the one named last changes fastest.
Arguments:
- inputs: bfloat16 [4, 4096, 768], P(None, 'dp'), may hold values from -6 to 6
- cotangent: bfloat16 [4, 4096, 768], P(None, 'dp'), may hold values from -6 to 6
- segments: int32 [4, 4096], P(None, 'dp'), may hold values from 0 to 95, never falling along the last dimension, each value on 1 to 128 neighbouring positions
- routes: int32 [2, 4, 4096, 1], P('pipe', None, 'dp'), may hold values from 0 to 1
- gain_attn: float32 [2, 768], P('pipe'), may hold values from 0.5 to 1.5
- w_qkv: bfloat16 [2, 3, 768, 768], P('pipe', None, None, 'tensor'), may hold values from -0.21875 to 0.21875
- rel_table: float32 [2, 32, 12], P('pipe', None, 'tensor'), may hold values from -3 to 3
- w_att_out: bfloat16 [2, 768, 768], P('pipe', 'tensor'), may hold values from -0.875 to 0.875
- gain_ffn: float32 [2, 768], P('pipe'), may hold values from 0.5 to 1.5
- router: float32 [2, 768, 2], P('pipe'), may hold values from -0.16 to 0.16
- w_in: bfloat16 [2, 2, 768, 3072], P('pipe', None, None, 'tensor'), may hold values from -0.21875 to 0.21875
- w_out: bfloat16 [2, 2, 3072, 768], P('pipe', None, 'tensor'), may hold values from -0.3125 to 0.3125
Outputs:
- section_out: bfloat16 [2, 4, 4096, 768], P('pipe', None, 'dp')
- input_grad: bfloat16 [2, 4, 4096, 768], P('pipe', None, 'dp')
- grad_gain_attn: float32 [2, 768], P('pipe')
- grad_qkv: float32 [2, 3, 768, 768], P('pipe', None, 'dp', 'tensor')
- grad_table: float32 [2, 32, 12], P('pipe', None, 'tensor')
- grad_att_out: float32 [2, 768, 768], P('pipe', 'tensor', 'dp')
- grad_gain_ffn: float32 [2, 768], P('pipe')
- grad_router: float32 [2, 768, 2], P('pipe')
- grad_in: float32 [2, 2, 768, 3072], P('pipe', None, 'dp', 'tensor')
- grad_out: float32 [2, 2, 3072, 768], P('pipe', None, 'tensor', 'dp')
Inputs may be any that keep to these rules, and one draw needn't show every extreme that they name: `segments`: segment numbers never fall along a micro-batch's tokens; each document holds 1 to 128 tokens and one holds exactly 128. `routes`: every expert is named by some token.
All inputs are finite; a program needn't handle non-finite values.
Results may differ from a plain program's by a relative error of at most 0.03.
Values may be sent and summed in bfloat16 or wider, within the bound.
A program may use at most 320 MiB of HBM per device.

v0:
```python
import jax
import jax.numpy as jnp
import numpy as np
from jax import lax
from jax.sharding import PartitionSpec as P

HEAD = 64


epsilon = 1e-06
highest = lax.Precision.HIGHEST
masked_value = -1e30


def copy_for_each(shard, axis):
    copies = jnp.broadcast_to(shard, (lax.axis_size(axis), *shard.shape))
    return lax.all_to_all(copies, axis, split_axis=0, concat_axis=0, tiled=True)


def of_everyone(shard, axis):
    everything = copy_for_each(shard, axis)
    return jnp.sum(everything, axis=0)


def taken_together(shard, axis):
    return copy_for_each(shard, axis).astype(jnp.float32).sum(axis=0)


def shifted(value, axis, steps):
    count = lax.axis_size(axis)
    initial, last = (max(0, -steps), min(count, count - steps))
    return lax.ppermute(value, axis, [(source, source + steps) for source in range(initial, last)])


def cut_along(shard, dim, devices):
    lengths = shard.shape
    parts = shard.reshape(*lengths[:dim], devices, lengths[dim] // devices, *lengths[dim + 1 :])
    return jnp.moveaxis(parts, dim, 0)


def one_scatter(arrays, axis, dims):
    devices = lax.axis_size(axis)
    parts = [cut_along(a, dim, devices) for a, dim in zip(arrays, dims)]
    lines = jnp.concatenate([b.reshape(devices, -1) for b in parts], axis=1)
    width = max(16, -(-lines.shape[1] // 1024) * 8)
    lines = jnp.pad(lines, ((0, 0), (0, width * 128 - lines.shape[1]))).reshape(-1, 128)
    flat, at, gathered = (lax.psum_scatter(lines, axis, tiled=True).reshape(-1), 0, [])
    for b in parts:
        part = b[0]
        gathered.append(flat[at : at + part.size].reshape(part.shape))
        at += part.size
    return tuple(gathered)


def together(arrays, axis):
    flat, at, gathered = (jnp.concatenate([a.reshape(-1) for a in arrays]), 0, [])
    running = of_everyone(flat, axis)
    for a in arrays:
        gathered.append(running[at : at + a.size].reshape(a.shape))
        at += a.size
    return tuple(gathered)


def bucket_onehot(length, buckets):
    places = np.arange(length)
    offset = places[None, :] - places[:, None]
    half = buckets // 2
    exact = half // 2
    upper = (offset > 0).astype(np.int64) * half
    distance = np.abs(offset)
    ratio = np.log(np.maximum(distance, 1) / exact) / np.log(128.0 / exact)
    far_bucket = np.minimum(
        exact + np.floor(ratio * (half - exact) + 1e-09).astype(np.int64), half - 1
    )
    bucket = upper + np.where(distance < exact, distance, far_bucket)
    return (bucket.reshape(-1)[None, :] == np.arange(buckets)[:, None]).astype(np.float32)


def rms_norm(values, gain):
    return values * lax.rsqrt(jnp.mean(values * values, axis=-1, keepdims=True) + epsilon) * gain


def attend_scores(query, keys, bias, segs):
    scores = (
        jnp.einsum("qhc,khc->hqk", query, keys, preferred_element_type=jnp.float32) * HEAD ** (-0.5)
        + bias
    )
    same = segs[:, None] == segs[None, :]
    return jnp.where(same[None], scores, masked_value)


def forward_layer(weights, bias, hidden, segs, route):
    gain_attn, w_qkv, rel_table, w_att_out, gain_ffn, router, w_in, w_out = weights
    length = hidden.shape[0]
    local_heads = w_qkv.shape[2] // HEAD
    normed = rms_norm(hidden, gain_attn).astype(jnp.bfloat16)
    projected = jnp.einsum("td,cdf->ctf", normed, w_qkv, preferred_element_type=jnp.float32).astype(
        jnp.bfloat16
    )
    split = projected.reshape(3, length, local_heads, HEAD)
    scores = attend_scores(split[0], split[1], bias, segs)
    peak = jnp.max(scores, axis=-1, keepdims=True)
    raised = jnp.exp(scores - peak)
    denominator = jnp.sum(raised, axis=-1, keepdims=True)
    probs = (raised / denominator).astype(jnp.bfloat16)
    log_total = peak + jnp.log(denominator)
    mixed = jnp.einsum("hqk,khc->qhc", probs, split[2], preferred_element_type=jnp.float32)
    mixed = mixed.reshape(length, -1).astype(jnp.bfloat16)
    attn_part = jnp.dot(mixed, w_att_out, preferred_element_type=jnp.float32)
    after = hidden + of_everyone(attn_part, "tensor")
    normed2 = rms_norm(after, gain_ffn).astype(jnp.bfloat16)
    gates = jax.nn.softmax(jnp.dot(normed2.astype(jnp.float32), router, precision=highest), axis=-1)
    picked = (route[:, None] == jnp.arange(router.shape[1])[None, :]).astype(jnp.float32)
    chosen = jnp.sum(gates * picked, axis=-1)
    inners = jnp.einsum("td,edf->etf", normed2, w_in, preferred_element_type=jnp.float32)
    actives = jax.nn.gelu(inners).astype(jnp.bfloat16)
    results = jnp.einsum("etf,efd->etd", actives, w_out, preferred_element_type=jnp.float32)
    weighting = (picked * chosen[:, None]).T
    expert_part = jnp.sum(weighting[:, :, None] * results, axis=0)
    output = after + taken_together(expert_part.astype(jnp.bfloat16), "tensor").astype(jnp.float32)
    kept = {
        "hidden": hidden,
        "segs": segs,
        "normed": normed,
        "projected": projected,
        "log_total": log_total,
        "mixed": mixed,
        "after": after,
        "normed2": normed2,
        "gates": gates,
        "picked": picked,
        "chosen": chosen,
        "inners": inners,
        "actives": actives,
        "results": results,
    }
    return (output, kept)


def expert_backward(weights, kept, d_out):
    gain_attn, w_qkv, rel_table, w_att_out, gain_ffn, router, w_in, w_out = weights
    picked = kept["picked"]
    chosen = kept["chosen"]
    weighting = (picked * chosen[:, None]).T
    d_result = (weighting[:, :, None] * d_out[None]).astype(jnp.bfloat16)
    g_out = jnp.einsum(
        "etf,etd->efd", kept["actives"], d_result, preferred_element_type=jnp.float32
    )
    d_active = jnp.einsum("etd,efd->etf", d_result, w_out, preferred_element_type=jnp.float32)
    unused, gelu_pull = jax.vjp(jax.nn.gelu, kept["inners"])
    d_inner = gelu_pull(d_active)[0].astype(jnp.bfloat16)
    g_in = jnp.einsum("td,etf->edf", kept["normed2"], d_inner, preferred_element_type=jnp.float32)
    d_normed_part = jnp.einsum("etf,edf->td", d_inner, w_in, preferred_element_type=jnp.float32)
    d_chosen_part = jnp.sum(picked.T * jnp.sum(kept["results"] * d_out[None], axis=-1), axis=0)
    factor = kept["gates"] * (picked - chosen[:, None])
    d_normed_part = d_normed_part + jnp.dot(
        d_chosen_part[:, None] * factor, router.T, precision=highest
    )
    summed, d_chosen = (
        taken_together(d_normed_part.astype(jnp.bfloat16), "tensor").astype(jnp.float32),
        taken_together(d_chosen_part.astype(jnp.bfloat16), "tensor").astype(jnp.float32),
    )
    d_logits = d_chosen[:, None] * factor
    g_router = jnp.dot(kept["normed2"].astype(jnp.float32).T, d_logits, precision=highest)
    unused, norm_pull = jax.vjp(rms_norm, kept["after"], gain_ffn)
    d_after, g_gain_ffn = norm_pull(summed)
    return (d_after + d_out, (g_gain_ffn, g_router, g_in, g_out))


def attention_backward(weights, bias, onehot_t, kept, d_after):
    gain_attn, w_qkv, rel_table, w_att_out, gain_ffn, router, w_in, w_out = weights
    length = d_after.shape[0]
    local_heads = w_qkv.shape[2] // HEAD
    d_attn = d_after.astype(jnp.bfloat16)
    g_att_out = jnp.einsum("tc,td->cd", kept["mixed"], d_attn, preferred_element_type=jnp.float32)
    d_mixed = jnp.einsum("td,cd->tc", d_attn, w_att_out, preferred_element_type=jnp.float32)
    d_mixed = d_mixed.astype(jnp.bfloat16).reshape(length, local_heads, HEAD)
    split = kept["projected"].reshape(3, length, local_heads, HEAD)
    scores = attend_scores(split[0], split[1], bias, kept["segs"])
    probs = jnp.exp(scores - kept["log_total"])
    d_values = jnp.einsum(
        "hqk,qhc->khc", probs.astype(jnp.bfloat16), d_mixed, preferred_element_type=jnp.float32
    )
    d_probs = jnp.einsum("qhc,khc->hqk", d_mixed, split[2], preferred_element_type=jnp.float32)
    d_scores = (probs * (d_probs - jnp.sum(probs * d_probs, axis=-1, keepdims=True))).astype(
        jnp.bfloat16
    )
    g_table = jnp.dot(
        onehot_t, d_scores.astype(jnp.float32).reshape(local_heads, -1).T, precision=highest
    )
    scale = HEAD ** (-0.5)
    d_query = (
        jnp.einsum("hqk,khc->qhc", d_scores, split[1], preferred_element_type=jnp.float32) * scale
    )
    d_keys = (
        jnp.einsum("hqk,qhc->khc", d_scores, split[0], preferred_element_type=jnp.float32) * scale
    )
    d_projected = jnp.stack([d_query, d_keys, d_values]).reshape(3, length, -1).astype(jnp.bfloat16)
    g_qkv = jnp.einsum(
        "td,ctf->cdf", kept["normed"], d_projected, preferred_element_type=jnp.float32
    )
    normed_part = jnp.einsum("ctf,cdf->td", d_projected, w_qkv, preferred_element_type=jnp.float32)
    d_normed = taken_together(normed_part.astype(jnp.bfloat16), "tensor").astype(jnp.float32)
    unused, norm_pull = jax.vjp(rms_norm, kept["hidden"], gain_attn)
    d_hidden, g_gain_attn = norm_pull(d_normed)
    return (d_hidden + d_after, (g_gain_attn, g_qkv, g_table, g_att_out))


def per_device(
    inputs,
    cotangent,
    segments,
    routes,
    gain_attn,
    w_qkv,
    rel_table,
    w_att_out,
    gain_ffn,
    router,
    w_in,
    w_out,
):
    weights = tuple(
        (
            item[0]
            for item in (gain_attn, w_qkv, rel_table, w_att_out, gain_ffn, router, w_in, w_out)
        )
    )
    micros = inputs.shape[0]
    length = inputs.shape[1]
    width = inputs.shape[2]
    first = lax.axis_index("pipe") == 0
    onehot_t = jnp.asarray(bucket_onehot(length, rel_table.shape[1]))
    bias = jnp.dot(weights[2].T, onehot_t, precision=highest).reshape(-1, length, length)

    def select(when_first, otherwise):
        return jax.tree.map(
            lambda left, right: jnp.where(first, left, right), when_first, otherwise
        )

    incoming = jnp.zeros((length, width), jnp.bfloat16)
    step_outputs = []
    step_kept = []
    for step in range(micros + 1):
        earlier = min(step, micros - 1)
        later = max(step - 1, 0)
        hidden = jnp.where(first, inputs[earlier], incoming).astype(jnp.float32)
        segs = jnp.where(first, segments[earlier], segments[later])
        route = jnp.where(first, routes[0, earlier, :, 0], routes[0, later, :, 0])
        output, kept = forward_layer(weights, bias, hidden, segs, route)
        sent = output.astype(jnp.bfloat16)
        step_outputs.append(sent)
        step_kept.append(kept)
        if step < micros:
            incoming = shifted(sent, "pipe", 1)
    by_micro = [select(step_kept[micro], step_kept[micro + 1]) for micro in range(micros)]
    section_out = jnp.stack(
        [jnp.where(first, step_outputs[micro], step_outputs[micro + 1]) for micro in range(micros)]
    )
    back_in = jnp.zeros((length, width), jnp.bfloat16)
    step_grads = []
    expert_totals = None
    attention_totals = None
    for step in range(micros + 1):
        later = min(step, micros - 1)
        earlier = max(step - 1, 0)
        kept = select(by_micro[earlier], by_micro[later])
        if step < micros:
            outer = cotangent[later]
        else:
            outer = jnp.zeros((length, width), jnp.bfloat16)
        d_out = jnp.where(first, back_in, outer).astype(jnp.float32)
        d_after, expert_grads = expert_backward(weights, kept, d_out)
        if expert_totals is None:
            expert_totals = expert_grads
        else:
            expert_totals = jax.tree.map(jnp.add, expert_totals, expert_grads)
        d_hidden, attention_grads = attention_backward(weights, bias, onehot_t, kept, d_after)
        if attention_totals is None:
            attention_totals = attention_grads
        else:
            attention_totals = jax.tree.map(jnp.add, attention_totals, attention_grads)
        sent = d_hidden.astype(jnp.bfloat16)
        step_grads.append(sent)
        if step < micros:
            back_in = shifted(sent, "pipe", -1)
    input_grad = jnp.stack(
        [jnp.where(first, step_grads[micro + 1], step_grads[micro]) for micro in range(micros)]
    )
    qkv_sum, att_sum, in_sum, out_sum = tuple(
        (
            part.astype(jnp.float32)
            for part in one_scatter(
                (
                    attention_totals[1].astype(jnp.bfloat16),
                    attention_totals[3].astype(jnp.bfloat16),
                    expert_totals[2].astype(jnp.bfloat16),
                    expert_totals[3].astype(jnp.bfloat16),
                ),
                "dp",
                (1, 1, 1, 2),
            )
        )
    )
    gain_a_sum, table_sum, gain_f_sum, router_sum = together(
        (attention_totals[0], attention_totals[2], expert_totals[0], expert_totals[1]), "dp"
    )
    return (
        section_out[None],
        input_grad[None],
        gain_a_sum[None],
        qkv_sum[None],
        table_sum[None],
        att_sum[None],
        gain_f_sum[None],
        router_sum[None],
        in_sum[None],
        out_sum[None],
    )


def solution(mesh):
    placed = (
        P(None, "dp", None),
        P(None, "dp", None),
        P(None, "dp"),
        P("pipe", None, "dp", None),
        P("pipe", None),
        P("pipe", None, None, "tensor"),
        P("pipe", None, "tensor"),
        P("pipe", "tensor", None),
        P("pipe", None),
        P("pipe", None, None),
        P("pipe", None, None, "tensor"),
        P("pipe", None, "tensor", None),
    )
    return jax.shard_map(
        per_device,
        mesh=mesh,
        in_specs=placed,
        out_specs=(
            P("pipe", None, "dp", None),
            P("pipe", None, "dp", None),
            P("pipe", None),
            P("pipe", None, "dp", "tensor"),
            P("pipe", None, "tensor"),
            P("pipe", "tensor", "dp"),
            P("pipe", None),
            P("pipe", None, None),
            P("pipe", None, "dp", "tensor"),
            P("pipe", None, "tensor", "dp"),
        ),
        check_vma=False,
    )
```

profile of v0, /device:TPU:0, one launch (start us, length us, event | category | flops | bytes accessed | tf_op | source)
XLA Modules:
  0.0 836.2 jit_solution(16770539328021351796)
XLA Ops:
  42.7 5.2 collective-permute-start
  62.6 5.3 all_to_all.137
  75.0 4.8 fusion.125
  81.5 5.5 multiply_reduce_fusion.4
  108.3 5.2 fusion.310
  118.6 4.6 collective-permute-start.1
  134.7 5.3 all_to_all.141
  147.9 5.0 fusion.133
  160.4 6.3 fusion.390
  188.6 5.2 fusion.287
  198.9 7.7 collective-permute-start.2
  210.7 6.2 fusion.388
  234.1 5.1 all_to_all.145
  251.8 9.0 %collective-permute-done.5 = bf16[128,768]{1,0:T(8,128)(2,1)S(1)} collective-permute-done((bf16[128,768]{1,0:T(8,128)(2,1)S(1)}, bf16[128,768]{1,0:T(8,128)(2,1)S(1)}, u32[]{:S(2)}, u32[]{:S(2)}) %collective-permute-start.5) | collective-permute-done | bytes 196640 | tf_op jit(solution)/shard_map/ppermute | solution.py:32
  263.9 5.3 fusion.285
  286.7 4.9 fusion.386
  332.7 4.4 all-to-all-start.8
  376.5 5.6 collective-permute-done.6
  407.7 5.1 fusion.283
  419.6 6.0 fusion.384
  451.4 7.5 reshape.1686
  458.9 7.3 fusion.160
  473.2 15.9 %add_convert_fusion.1 = bf16[2,1536,768]{1,2,0:T(8,128)(2,1)} fusion(f32[2,1536,768]{1,2,0:T(8,128)} %fusion.384, f32[2,1536,768]{1,2,0:T(8,128)} %fusion.386, f32[2,1536,768]{1,2,0:T(8,128)} %fusion.390, f32[2,1536,768]{1,2,0:T(8,128)} %fusion.388, bf16[2,128,1536]{2,1,0:T(8,128)(2,1)} %copy-done.99, bf16[128,768]{1,0:T(8,128)(2,1)S(1)} %copy-done.106), kind=kOutput, calls=%fused_computation.2 | convolution fusion | flops 615776256 | bytes 43450368 | tf_op jit(solution)/shard_map/td,etf->edf/dot_general | solution.py:152
  491.9 4.7 copy.600
  496.7 16.3 %add_convert_fusion = bf16[2,1536,768]{1,2,0:T(8,128)(2,1)} fusion(f32[2,1536,768]{1,2,0:T(8,128)} %fusion.283, f32[2,1536,768]{1,2,0:T(8,128)} %fusion.285, f32[2,1536,768]{1,2,0:T(8,128)} %fusion.310, f32[2,1536,768]{1,2,0:T(8,128)} %fusion.287, f32[128,768]{1,0:T(8,128)S(1)} %copy-done.69, f32[2,128]{1,0:T(2,128)S(1)} %get-tuple-element.223, ...), kind=kOutput, calls=%fused_computation.1 | convolution fusion | flops 620101632 | bytes 45220864 | tf_op jit(solution)/shard_map/etf,etd->efd/dot_general | solution.py:146
  513.0 19.9 %copy.543 = bf16[2,1536,32,24]{3,1,0,2:T(8,128)(2,1)} copy(bf16[2,1536,32,24]{1,3,2,0:T(8,128)(2,1)} %bitcast.783) | data formatting | bytes 9437184 | tf_op jit(solution)/shard_map/reshape | solution.py:37
  532.9 69.8 %reshape.1690 = bf16[32,73728]{1,0:T(8,128)(2,1)} reshape(bf16[32,2,1536,24]{3,2,1,0:T(8,128)(2,1)} %bitcast.772) | data formatting | bytes 9437184 | tf_op jit(solution)/shard_map/reshape | solution.py:44
  602.7 13.7 %pad_maximum_fusion = bf16[32,184320]{1,0:T(8,128)(2,1)} fusion(bf16[32,73728]{1,0:T(8,128)(2,1)} %reshape.1690, bf16[32,73728]{1,0:T(8,128)(2,1)} %bitcast.785, bf16[32,9216]{1,0:T(8,128)(2,1)} %reshape.1686, bf16[32,27648]{1,0:T(8,128)(2,1)} %bitcast.787), kind=kLoop, calls=%fused_computation | loop fusion | flops 47185920 | bytes 23592960 | tf_op jit(solution)/shard_map/concatenate | solution.py:44
  616.4 11.5 %reshape.1691 = bf16[46080,128]{1,0:T(8,128)(2,1)} reshape(bf16[32,184320]{1,0:T(8,128)(2,1)} %pad_maximum_fusion) | data formatting | bytes 23592960 | tf_op jit(solution)/shard_map/reshape | solution.py:46
  679.0 8.4 %all-to-all-start.25 = ((f32[32,1,3264]{2,1,0:T(1,128)}), f32[32,1,3264]{2,1,0:T(1,128)}, u32[]{:S(2)}, u32[]{:S(2)}) async-start(f32[32,1,3264]{2,1,0:T(1,128)} %broadcast_in_dim.368), calls=%async_computation.25 | async-start | bytes 851968 | tf_op jit(solution)/shard_map/all_to_all | solution.py:17
  692.0 10.8 %all-to-all-done.25 = f32[32,1,3264]{2,1,0:T(1,128)} async-done(((f32[32,1,3264]{2,1,0:T(1,128)}), f32[32,1,3264]{2,1,0:T(1,128)}, u32[]{:S(2)}, u32[]{:S(2)}) %all-to-all-start.25) | async-done | bytes 417824 | tf_op jit(solution)/shard_map/all_to_all | solution.py:17
  707.2 112.3 %reduce-scatter.2.cloned.1.call-done = bf16[1440,128]{1,0:T(8,128)(2,1)} async-done(((bf16[46080,128]{1,0:T(8,128)(2,1)}), bf16[1440,128]{1,0:T(8,128)(2,1)}) %reduce-scatter.2.cloned.1.call-update) | async-done | bytes 368656 | tf_op jit(solution)/shard_map/reduce_scatter | solution.py:47
  (1104 shorter events, 406.8 us)
Async XLA Ops:
  21.5 6.4 all-to-all-start
  38.4 14.4 %copy-start.280 = (s32[128]{0:T(128)S(1)}, s32[128]{0:T(128)}, u32[]{:S(2)}) copy-start(s32[128]{0:T(128)} %get-tuple-element.206) | copy-start | bytes 1540
  42.7 10.7 %collective-permute-start = (bf16[128,768]{1,0:T(8,128)(2,1)S(1)}, bf16[128,768]{1,0:T(8,128)(2,1)S(1)}, u32[]{:S(2)}, u32[]{:S(2)}) collective-permute-start(bf16[128,768]{1,0:T(8,128)(2,1)S(1)} %add_convert_fusion.7), channel_id=1, source_target_pairs={{0,64},{1,65},{2,66},{3,67},{4,68},{5,69},{6,70},{7,71},{8,72},{9,... | collective-permute-start | bytes 589832 | tf_op jit(solution)/shard_map/ppermute | solution.py:32
  48.5 224.4 %copy-start.175 = (s32[128]{0:T(128)}, s32[128]{0:T(128)S(1)}, u32[]{:S(2)}) copy-start(s32[128]{0:T(128)S(1)} %get-tuple-element.276) | copy-start | bytes 1540
  54.2 287.0 %copy-start.8 = (bf16[128,768]{1,0:T(8,128)(2,1)}, bf16[128,768]{1,0:T(8,128)(2,1)S(1)}, u32[]{:S(2)}) copy-start(bf16[128,768]{1,0:T(8,128)(2,1)S(1)} %get-tuple-element.150) | copy-start | bytes 589828
  73.9 19.9 %copy-start.184 = (f32[128,2]{0,1:T(2,128)}, f32[128,2]{0,1:T(2,128)S(1)}, u32[]{:S(2)}) copy-start(f32[128,2]{0,1:T(2,128)S(1)} %get-tuple-element.149) | copy-start | bytes 3076
  118.6 9.0 %collective-permute-start.1 = (bf16[128,768]{1,0:T(8,128)(2,1)S(1)}, bf16[128,768]{1,0:T(8,128)(2,1)S(1)}, u32[]{:S(2)}, u32[]{:S(2)}) collective-permute-start(bf16[128,768]{1,0:T(8,128)(2,1)S(1)} %get-tuple-element.108), channel_id=1, source_target_pairs={{0,64},{1,65},{2,66},{3,67},{4,68},{5,69},{6,70},{7,71},{8,72},{9,... | collective-permute-start | bytes 589832 | tf_op jit(solution)/shard_map/ppermute | solution.py:32
  128.5 212.6 %copy-start.4 = (bf16[128,768]{1,0:T(8,128)(2,1)}, bf16[128,768]{1,0:T(8,128)(2,1)S(1)}, u32[]{:S(2)}) copy-start(bf16[128,768]{1,0:T(8,128)(2,1)S(1)} %get-tuple-element.144) | copy-start | bytes 589828
  145.8 64.9 %copy-start.108 = (bf16[128,768]{1,0:T(8,128)(2,1)}, bf16[128,768]{1,0:T(8,128)(2,1)S(1)}, u32[]{:S(2)}) copy-start(bf16[128,768]{1,0:T(8,128)(2,1)S(1)} %get-tuple-element.92) | copy-start | bytes 589828
  154.3 12.3 %collective-permute-start.4 = (bf16[128,768]{1,0:T(8,128)(2,1)}, bf16[128,768]{1,0:T(8,128)(2,1)}, u32[]{:S(2)}, u32[]{:S(2)}) collective-permute-start(bf16[128,768]{1,0:T(8,128)(2,1)} %fusion.313), channel_id=1, source_target_pairs={{64,0},{65,1},{66,2},{67,3},{68,4},{69,5},{70,6},{71,7},{72,8},{73... | collective-permute-start | bytes 589832 | tf_op jit(solution)/shard_map/ppermute | solution.py:32
  198.9 25.5 %collective-permute-start.2 = (bf16[128,768]{1,0:T(8,128)(2,1)}, bf16[128,768]{1,0:T(8,128)(2,1)}, u32[]{:S(2)}, u32[]{:S(2)}) collective-permute-start(bf16[128,768]{1,0:T(8,128)(2,1)} %get-tuple-element.110), channel_id=1, source_target_pairs={{0,64},{1,65},{2,66},{3,67},{4,68},{5,69},{6,70},{7,71},{8,72},{9,... | collective-permute-start | bytes 589832 | tf_op jit(solution)/shard_map/ppermute | solution.py:32
  242.7 40.2 %copy-start.32 = (f32[128,768]{1,0:T(8,128)}, f32[128,768]{1,0:T(8,128)S(1)}, u32[]{:S(2)}) copy-start(f32[128,768]{1,0:T(8,128)S(1)} %get-tuple-element.135) | copy-start | bytes 1179652
  243.1 43.5 %copy-start.114 = (bf16[128,768]{1,0:T(8,128)(2,1)}, bf16[128,768]{1,0:T(8,128)(2,1)S(1)}, u32[]{:S(2)}) copy-start(bf16[128,768]{1,0:T(8,128)(2,1)S(1)} %get-tuple-element.90) | copy-start | bytes 589828
  243.5 29.5 %copy-start.207 = (f32[128,2]{0,1:T(2,128)}, f32[128,2]{0,1:T(2,128)S(1)}, u32[]{:S(2)}) copy-start(f32[128,2]{0,1:T(2,128)S(1)} %get-tuple-element.137) | copy-start | bytes 3076
  243.5 29.4 %copy-start.239 = (f32[128]{0:T(128)}, f32[128]{0:T(128)S(1)}, u32[]{:S(2)}) copy-start(f32[128]{0:T(128)S(1)} %broadcast_select_fusion.79) | copy-start | bytes 1540
  243.5 18.2 %slice-start.14 = ((s8[4718592]{0:T(1024)(128)(4,1)}), s8[4194304]{0:T(1024)(128)(4,1)S(1)}, s32[]{:S(2)}) async-start(s8[4718592]{0:T(1024)(128)(4,1)} %bitcast.777), calls=%async_computation.42 | async-start | bytes 8388608
  243.6 18.2 %slice-start.15 = ((s8[4718592]{0:T(1024)(128)(4,1)}), s8[524288]{0:T(1024)(128)(4,1)S(1)}, s32[]{:S(2)}) async-start(s8[4718592]{0:T(1024)(128)(4,1)} %bitcast.777), calls=%async_computation.43 | async-start | bytes 1048576
  247.3 16.5 %copy-start.42 = (bf16[2,128,1536]{2,1,0:T(8,128)(2,1)}, bf16[2,128,1536]{2,1,0:T(8,128)(2,1)S(1)}, u32[]{:S(2)}) copy-start(bf16[2,128,1536]{2,1,0:T(8,128)(2,1)S(1)} %get-tuple-element.257) | copy-start | bytes 2359300
  247.3 21.9 %copy-start.306 = (f32[2,128,1536]{2,1,0:T(8,128)}, f32[2,128,1536]{2,1,0:T(8,128)S(1)}, u32[]{:S(2)}) copy-start(f32[2,128,1536]{2,1,0:T(8,128)S(1)} %get-tuple-element.258) | copy-start | bytes 4718596
  247.3 14.5 %copy-start.48 = (f32[2,128,768]{2,1,0:T(8,128)S(1)}, f32[2,128,768]{2,1,0:T(8,128)}, u32[]{:S(2)}) copy-start(f32[2,128,768]{2,1,0:T(8,128)} %get-tuple-element.250) | copy-start | bytes 2359300
  247.3 14.5 %copy-start.51 = (f32[2,128,768]{2,1,0:T(8,128)S(1)}, f32[2,128,768]{2,1,0:T(8,128)}, u32[]{:S(2)}) copy-start(f32[2,128,768]{2,1,0:T(8,128)} %get-tuple-element.239) | copy-start | bytes 2359300
  250.5 10.3 %collective-permute-start.5 = (bf16[128,768]{1,0:T(8,128)(2,1)S(1)}, bf16[128,768]{1,0:T(8,128)(2,1)S(1)}, u32[]{:S(2)}, u32[]{:S(2)}) collective-permute-start(bf16[128,768]{1,0:T(8,128)(2,1)S(1)} %get-tuple-element.96), channel_id=1, source_target_pairs={{64,0},{65,1},{66,2},{67,3},{68,4},{69,5},{70,6},{71,7},{72,8},{73... | collective-permute-start | bytes 589832 | tf_op jit(solution)/shard_map/ppermute | solution.py:32
  284.7 8.9 %collective-permute-start.3 = (bf16[128,768]{1,0:T(8,128)(2,1)}, bf16[128,768]{1,0:T(8,128)(2,1)}, u32[]{:S(2)}, u32[]{:S(2)}) collective-permute-start(bf16[128,768]{1,0:T(8,128)(2,1)} %get-tuple-element.112), channel_id=1, source_target_pairs={{0,64},{1,65},{2,66},{3,67},{4,68},{5,69},{6,70},{7,71},{8,72},{9,... | collective-permute-start | bytes 589832 | tf_op jit(solution)/shard_map/ppermute | solution.py:32
  324.6 6.1 all-to-all-start.15
  332.7 6.5 all-to-all-start.8
  337.1 482.4 %reduce-scatter.2.cloned.1.call-start = ((), (), s32[]{:S(2)}) async-start(), calls=%async_computation.27 | async-start | bytes 12165120 | tf_op jit(solution)/shard_map/reduce_scatter | solution.py:47
  351.6 31.5 %slice-start.16 = ((s8[4718592]{0:T(1024)(128)(4,1)}), s8[524288]{0:T(1024)(128)(4,1)S(1)}, s32[]{:S(2)}) async-start(s8[4718592]{0:T(1024)(128)(4,1)} %bitcast.779), calls=%async_computation.44 | async-start | bytes 1048576
  368.6 14.5 %slice-start.17 = ((s8[4718592]{0:T(1024)(128)(4,1)}), s8[4194304]{0:T(1024)(128)(4,1)S(1)}, s32[]{:S(2)}) async-start(s8[4718592]{0:T(1024)(128)(4,1)} %bitcast.779), calls=%async_computation.45 | async-start | bytes 8388608
  371.5 10.6 %collective-permute-start.6 = (bf16[128,768]{1,0:T(8,128)(2,1)S(1)}, bf16[128,768]{1,0:T(8,128)(2,1)S(1)}, u32[]{:S(2)}, u32[]{:S(2)}) collective-permute-start(bf16[128,768]{1,0:T(8,128)(2,1)S(1)} %get-tuple-element.98), channel_id=1, source_target_pairs={{64,0},{65,1},{66,2},{67,3},{68,4},{69,5},{70,6},{71,7},{72,8},{73... | collective-permute-start | bytes 589832 | tf_op jit(solution)/shard_map/ppermute | solution.py:32
  418.2 10.3 %collective-permute-start.7 = (bf16[128,768]{1,0:T(8,128)(2,1)S(1)}, bf16[128,768]{1,0:T(8,128)(2,1)S(1)}, u32[]{:S(2)}, u32[]{:S(2)}) collective-permute-start(bf16[128,768]{1,0:T(8,128)(2,1)S(1)} %get-tuple-element.100), channel_id=1, source_target_pairs={{64,0},{65,1},{66,2},{67,3},{68,4},{69,5},{70,6},{71,7},{72,8},{73... | collective-permute-start | bytes 589832 | tf_op jit(solution)/shard_map/ppermute | solution.py:32
  672.0 5.9 all-to-all-start.9
  679.0 23.8 %all-to-all-start.25 = ((f32[32,1,3264]{2,1,0:T(1,128)}), f32[32,1,3264]{2,1,0:T(1,128)}, u32[]{:S(2)}, u32[]{:S(2)}) async-start(f32[32,1,3264]{2,1,0:T(1,128)} %broadcast_in_dim.368), calls=%async_computation.25 | async-start | bytes 851968 | tf_op jit(solution)/shard_map/all_to_all | solution.py:17
  (314 other events, 1478.1 us)
Sparse Core Ops, SparseCore 0:
  628.1 191.4 reduce-scatter.1
where the time goes:
time: 848 us; the launch traced here: 836 us
  matrix products  222 us (26%)
  local copies, waits for them, and re-layouts  217 us (26%)
  waiting for transfers between devices  142 us (17%)
  other arithmetic  98 us (12%)
  blocking collectives  88.1 us (10%)
  starting transfers between devices  50.5 us (6%)
  between operations  19.4 us (2%)
    reduce_scatter x1, waiting for transfers between devices, one_scatter(): lax.psum_scatter(lines, axis, tiled=True).reshape(-1)  112 us
    all_to_all x21, blocking collectives, copy_for_each(): return lax.all_to_all(copies, axis, split_axis=0, concat_axis=0, tiled=True)  88.1 us
    reshape x2, local copies, waits for them, and re-layouts, one_scatter(): lines = jnp.concatenate([b.reshape(devices, -1) for b in parts], axis=1)  77.3 us
    dot_general x5, matrix products, expert_backward(): jnp.einsum('td,etf->edf', kept['normed2'], d_inner, preferred_element_typ...  39.3 us
    dot_general x5, matrix products, expert_backward(): jnp.einsum('etf,etd->efd', kept['actives'], d_result, preferred_element_t...  37.1 us
    all_to_all x5, starting transfers between devices, copy_for_each(): return lax.all_to_all(copies, axis, split_axis=0, concat_axis=0, tiled=True)  25.5 us
    ppermute x8, starting transfers between devices, shifted(): lax.ppermute(value, axis, [(source, source + steps) for source in range(i...  24.9 us
    reshape x2, local copies, waits for them, and re-layouts, cut_along(): shard.reshape(*lengths[:dim], devices, lengths[dim] // devices, *lengths[...  22.8 us
  transfers between devices with their start and end apart: 14, of which 9 were waited for; matrix products, arithmetic and copies ran while one was open for 10% of the time, Pallas kernels for 0%

commit v1 on v0

v1 whole, which is shorter than its diff:
```python
import functools

import jax
import jax.numpy as jnp
import numpy as np
from jax import lax
from jax.experimental import pallas as pl
from jax.experimental.pallas import tpu as pltpu
from jax.sharding import PartitionSpec as P

HEAD = 64
LEN = 128
PAIRS = 3
SEQS = 2
epsilon = 1e-06
masked_value = -1e30
F32 = jnp.float32
BF16 = jnp.bfloat16
NT = (((1,), (1,)), ((), ()))
TN = (((0,), (0,)), ((), ()))


def far_limits(buckets):
    half = buckets // 2
    exact = half // 2
    distance = np.arange(LEN)
    ratio = np.log(np.maximum(distance, 1) / exact) / np.log(128.0 / exact)
    bucket = np.minimum(exact + np.floor(ratio * (half - exact) + 1e-09).astype(np.int64), half - 1)
    bucket = np.where(distance < exact, distance, bucket)
    return [int(np.argmax(bucket >= b)) for b in range(1, half) if np.any(bucket >= b)]


def bucket_map(buckets):
    query = lax.broadcasted_iota(jnp.int32, (LEN, LEN), 0)
    key = lax.broadcasted_iota(jnp.int32, (LEN, LEN), 1)
    offset = key - query
    distance = jnp.abs(offset)
    bucket = jnp.where(offset > 0, buckets // 2, 0)
    for limit in far_limits(buckets):
        bucket = bucket + jnp.where(distance >= limit, 1, 0)
    return bucket


def dot(a, b, dims=None):
    if dims is None:
        return jnp.dot(a, b, preferred_element_type=F32)
    return lax.dot_general(a, b, dims, preferred_element_type=F32)


def over_rows(values):
    return jnp.sum(values, axis=0, keepdims=True)


def over_lanes(values):
    return jnp.sum(values, axis=1, keepdims=True)


def kernel(
    x_hbm, dy_hbm, segs, routes, gain_a, table, gain_f, rdiff, wqkv_hbm, watt_hbm, win_hbm, wout_hbm,
    sec, dgrad, grads, small, tables,
    wqkv, watt, win, wout, hs, dys, xt, nt, rt, at, proj, probs, mixed, after, slope, act2, back2,
    result, chosens, dproj, send, recv, bias, dsum,
    load_sem, out_sem, in_sem, pipe_out, pipe_in,
):
    pipe = lax.axis_index("pipe")
    tensor = lax.axis_index("tensor")
    first = pipe == 0
    last = pipe == 1
    chunks, rows, width = hs.shape
    hidden = slope.shape[-1]
    step = 512
    buckets = table.shape[0]

    loads = [
        pltpu.make_async_copy(source, target, load_sem.at[i])
        for i, (source, target) in enumerate(
            ((wqkv_hbm, wqkv), (watt_hbm, watt), (win_hbm, win), (wout_hbm, wout))
        )
    ]
    load_x = pltpu.make_async_copy(x_hbm, hs, load_sem.at[4])
    load_dy = pltpu.make_async_copy(dy_hbm, dys, load_sem.at[4])

    @pl.when(first)
    def _():
        load_x.start()

    @pl.when(last)
    def _():
        load_dy.start()

    for load in loads:
        load.start()

    barrier = pltpu.get_barrier_semaphore()
    pl.semaphore_signal(barrier, inc=1, device_id={"tensor": 1 - tensor}, device_id_type=pl.DeviceIdType.MESH)
    pl.semaphore_signal(barrier, inc=1, device_id={"pipe": 1 - pipe}, device_id_type=pl.DeviceIdType.MESH)
    pl.semaphore_wait(barrier, 2)

    def to_other_core(slot):
        return pltpu.make_async_remote_copy(
            src_ref=send.at[slot], dst_ref=recv.at[slot], send_sem=out_sem.at[slot],
            recv_sem=in_sem.at[slot], device_id={"tensor": 1 - tensor},
            device_id_type=pl.DeviceIdType.MESH,
        )

    def to_other_section(source, target, slot):
        return pltpu.make_async_remote_copy(
            src_ref=source, dst_ref=target, send_sem=pipe_out.at[slot],
            recv_sem=pipe_in.at[slot], device_id={"pipe": 1 - pipe},
            device_id_type=pl.DeviceIdType.MESH,
        )

    def forward_copy(c):
        return to_other_section(sec.at[c], hs.at[c], c)

    def backward_copy(c):
        return to_other_section(dgrad.at[c], dys.at[c], chunks + c)

    def exchanged(slot, part):
        send[slot] = part.astype(BF16)
        copy = to_other_core(slot)
        copy.start()
        copy.wait()
        return send[slot].astype(F32) + recv[slot].astype(F32)

    bucket = bucket_map(buckets)
    lane = lax.broadcasted_iota(jnp.int32, (LEN, LEN), 1)
    upper = lane >= HEAD
    bias[...] = jnp.zeros_like(bias)
    dsum[...] = jnp.zeros_like(dsum)
    small[...] = jnp.zeros_like(small)

    def add_bias(b, carry):
        hit = bucket == b
        for pair in range(PAIRS):
            for side in range(2):
                at_lanes = pl.ds(side * LEN, LEN)
                bias[pair, :, at_lanes] = jnp.where(hit, table[b, 2 * pair + side], bias[pair, :, at_lanes])
        return carry

    lax.fori_loop(0, buckets, add_bias, 0)

    def stacked(values):
        zero = jnp.zeros_like(values)
        return jnp.concatenate([jnp.where(upper, zero, values), jnp.where(upper, values, zero)], axis=0)

    def unstacked(values):
        return jnp.where(upper, values[LEN:], values[:LEN])

    def per_head(values, reduce):
        left = reduce(values[:, :LEN], axis=1, keepdims=True)
        right = reduce(values[:, LEN:], axis=1, keepdims=True)
        return jnp.concatenate(
            [jnp.broadcast_to(left, (LEN, LEN)), jnp.broadcast_to(right, (LEN, LEN))], axis=1
        )

    for load in loads:
        load.wait()

    @pl.when(first)
    def _():
        load_x.wait()

    def forward(c, carry):
        @pl.when(last)
        def _():
            forward_copy(c).wait_recv()

        spot = pl.multiple_of(c * rows, rows)
        here = pl.ds(spot, rows)
        h = hs[c].astype(F32)
        scale = lax.rsqrt(jnp.mean(h * h, axis=1, keepdims=True) + epsilon)
        normed = (h * scale * gain_a[...]).astype(BF16)
        xt[:, here] = normed.T
        for part in range(3):
            proj[part, here, :] = dot(normed, wqkv[part]).astype(BF16)
        for s in range(SEQS):
            seq = pl.ds(pl.multiple_of(spot + s * LEN, LEN), LEN)
            along = jnp.broadcast_to(segs[pl.ds(c * SEQS + s, 1), :].astype(F32), (LEN, LEN))
            same = along == along.T
            same = jnp.concatenate([same, same], axis=1)
            for pair in range(PAIRS):
                lanes = pl.ds(pair * LEN, LEN)
                query = proj[0, seq, lanes]
                keys = stacked(proj[1, seq, lanes])
                values = stacked(proj[2, seq, lanes])
                scores = dot(query, keys, NT) * HEAD ** (-0.5) + bias[pair]
                scores = jnp.where(same, scores, masked_value)
                raised = jnp.exp(scores - per_head(scores, jnp.max))
                prob = raised / per_head(raised, jnp.sum)
                probs[c * SEQS + s, pair] = prob
                mixed[seq, lanes] = dot(prob.astype(BF16), values).astype(BF16)
        a = h + exchanged(4 * c, dot(mixed[here, :], watt[...]))
        after[here, :] = a
        scale = lax.rsqrt(jnp.mean(a * a, axis=1, keepdims=True) + epsilon)
        normed2 = (a * scale * gain_f[...]).astype(BF16)
        nt[:, here] = normed2.T
        route = routes[c]
        sign = (1 - 2 * route).astype(F32)
        logit = over_lanes(normed2.astype(F32) * rdiff[...])
        chosen = 1.0 / (1.0 + jnp.exp(-sign * logit))
        chosens[c] = chosen
        to_zero = (route == 0).astype(BF16)
        to_one = (route == 1).astype(BF16)
        doubled = jnp.concatenate([normed2 * to_zero, normed2 * to_one], axis=1)

        def inner_tile(n, carry):
            lanes = pl.ds(pl.multiple_of(n * step, step), step)
            inner = dot(doubled, win[:, lanes])
            squared = inner * inner
            root = np.sqrt(2 / np.pi).astype(np.float32)
            bend = jnp.tanh(root * inner * (1.0 + 0.044715 * squared))
            slope[here, lanes] = 0.5 * (1.0 + bend) + 0.5 * inner * (1.0 - bend * bend) * root * (
                1.0 + 3 * 0.044715 * squared
            )
            active = (0.5 * inner * (1.0 + bend)).astype(BF16)
            act2[here, lanes] = active * to_zero
            act2[here, pl.ds(pl.multiple_of(hidden + n * step, step), step)] = active * to_one
            return carry

        lax.fori_loop(0, hidden // step, inner_tile, 0)
        total = exchanged(4 * c + 1, dot(act2[here, :], wout[...]))
        result[here, :] = total
        sec[c] = (after[here, :] + chosen * total).astype(BF16)

        @pl.when(first)
        def _():
            forward_copy(c).start()

        return carry

    lax.fori_loop(0, chunks, forward, 0)

    @pl.when(last)
    def _():
        load_dy.wait()

    def backward(c, carry):
        @pl.when(first)
        def _():
            backward_copy(c).wait_recv()

        spot = pl.multiple_of(c * rows, rows)
        here = pl.ds(spot, rows)
        dy = dys[c].astype(F32)
        route = routes[c]
        sign = (1 - 2 * route).astype(F32)
        to_zero = (route == 0).astype(BF16)
        to_one = (route == 1).astype(BF16)
        chosen = chosens[c]
        d_logit = sign * over_lanes(dy * result[here, :]) * chosen * (1.0 - chosen)
        d_result = (chosen * dy).astype(BF16)
        rt[:, here] = d_result.T
        zero_part = d_result * to_zero
        one_part = d_result * to_one

        def active_tile(n, carry):
            low = pl.multiple_of(n * step, step)
            high = pl.multiple_of(hidden + n * step, step)
            d_active = dot(zero_part, wout[pl.ds(low, step), :], NT) + dot(
                one_part, wout[pl.ds(high, step), :], NT
            )
            d_inner = (d_active * slope[here, pl.ds(low, step)]).astype(BF16)
            back2[here, pl.ds(low, step)] = d_inner * to_zero
            back2[here, pl.ds(high, step)] = d_inner * to_one
            return carry

        lax.fori_loop(0, hidden // step, active_tile, 0)
        d_normed2 = dot(back2[here, :hidden], win[:width, :], NT) + dot(
            back2[here, hidden:], win[width:, :], NT
        )
        d_normed2 = exchanged(4 * c + 2, d_normed2) + d_logit * rdiff[...]
        a = after[here, :]
        scale = lax.rsqrt(jnp.mean(a * a, axis=1, keepdims=True) + epsilon)
        plain = a * scale
        normed2 = (plain * gain_f[...]).astype(BF16).astype(F32)
        small[1:2, :] += over_rows(d_normed2 * plain)
        small[2:3, :] += over_rows(normed2 * d_logit)
        pulled = d_normed2 * gain_f[...]
        d_after = dy + scale * (pulled - plain * jnp.mean(pulled * plain, axis=1, keepdims=True))
        after[here, :] = d_after
        d_attn = d_after.astype(BF16)
        at[:, here] = d_attn.T
        d_mixed = dot(d_attn, watt[...], NT).astype(BF16)
        for s in range(SEQS):
            seq = pl.ds(pl.multiple_of(spot + s * LEN, LEN), LEN)
            for pair in range(PAIRS):
                lanes = pl.ds(pair * LEN, LEN)
                query = proj[0, seq, lanes]
                keys = stacked(proj[1, seq, lanes])
                values = stacked(proj[2, seq, lanes])
                prob = probs[c * SEQS + s, pair]
                d_mix = d_mixed[s * LEN : (s + 1) * LEN, pair * LEN : (pair + 1) * LEN]
                product = prob * dot(d_mix, values, NT)
                d_scores = (product - prob * per_head(product, jnp.sum)).astype(BF16)
                dsum[pair] += d_scores.astype(F32)
                dproj[seq, pl.ds(pair * LEN, LEN)] = (dot(d_scores, keys) * HEAD ** (-0.5)).astype(BF16)
                d_keys = unstacked(dot(d_scores, query, TN)) * HEAD ** (-0.5)
                dproj[seq, pl.ds((PAIRS + pair) * LEN, LEN)] = d_keys.astype(BF16)
                d_values = unstacked(dot(prob.astype(BF16), d_mix, TN))
                dproj[seq, pl.ds((2 * PAIRS + pair) * LEN, LEN)] = d_values.astype(BF16)
        part = PAIRS * LEN
        d_normed = dot(dproj[here, :part], wqkv[0], NT)
        d_normed = d_normed + dot(dproj[here, part : 2 * part], wqkv[1], NT)
        d_normed = d_normed + dot(dproj[here, 2 * part :], wqkv[2], NT)
        d_normed = exchanged(4 * c + 3, d_normed)
        h = hs[c].astype(F32)
        scale = lax.rsqrt(jnp.mean(h * h, axis=1, keepdims=True) + epsilon)
        plain = h * scale
        small[0:1, :] += over_rows(d_normed * plain)
        pulled = d_normed * gain_a[...]
        d_hidden = after[here, :] + scale * (
            pulled - plain * jnp.mean(pulled * plain, axis=1, keepdims=True)
        )
        dgrad[c] = d_hidden.astype(BF16)

        @pl.when(last)
        def _():
            backward_copy(c).start()

        return carry

    lax.fori_loop(0, chunks, backward, 0)

    def keep(tile, left, right):
        shards, double, _ = grads.shape
        both = [side.reshape(shards, double // 2, LEN) for side in (left, right)]
        grads[:, :, pl.ds(pl.multiple_of(tile * LEN, LEN), LEN)] = jnp.concatenate(both, axis=1).astype(BF16)

    def product_tiles(tile, lefts, rights, count):
        def one(n, carry):
            lanes = pl.ds(pl.multiple_of(n * 2 * LEN, 2 * LEN), 2 * LEN)
            made = dot(lefts[...], rights[:, lanes])
            keep(tile + n, made[:, :LEN], made[:, LEN:])
            return carry

        lax.fori_loop(0, count, one, 0)

    out_tiles = 2 * hidden // (2 * LEN)
    product_tiles(0, rt, act2, out_tiles)
    product_tiles(out_tiles, nt, back2, out_tiles)
    product_tiles(2 * out_tiles, xt, dproj, 4)
    keep(2 * out_tiles + 4, dot(xt[...], dproj[:, 8 * LEN :]), dot(at[...], mixed[:, 2 * LEN :]))
    made = dot(at[...], mixed[:, : 2 * LEN])
    keep(2 * out_tiles + 5, made[:, :LEN], made[:, LEN:])

    def table_rows(b, carry):
        hit = bucket == b
        for pair in range(PAIRS):
            for side in range(2):
                picked = jnp.where(hit, dsum[pair, :, pl.ds(side * LEN, LEN)], 0.0)
                tables[2 * pair + side, pl.ds(b, 1), :] = over_rows(picked)
        return carry

    lax.fori_loop(0, buckets, table_rows, 0)

    def finish(c, carry):
        @pl.when(first)
        def _():
            forward_copy(c).wait_send()

        @pl.when(last)
        def _():
            backward_copy(c).wait_send()

        return carry

    lax.fori_loop(0, chunks, finish, 0)


def local_pass(inputs, cotangent, segments, routes, gain_attn, w_qkv, rel_table, w_att_out, gain_ffn, router, w_in, w_out, shards):
    micros, length, width = inputs.shape
    chunks = micros // SEQS
    rows = SEQS * length
    tokens = micros * length
    experts, _, hidden = w_in.shape
    heads = w_att_out.shape[0]
    buckets = rel_table.shape[0]
    columns = (3 * heads + heads + 2 * experts * hidden) // 2
    vmem = pl.BlockSpec(memory_space=pltpu.VMEM)
    smem = pl.BlockSpec(memory_space=pltpu.SMEM)
    anywhere = pl.BlockSpec(memory_space=pl.ANY)
    slots = 4 * chunks
    scratch = [
        pltpu.VMEM(w_qkv.shape, BF16),
        pltpu.VMEM(w_att_out.shape, BF16),
        pltpu.VMEM((experts * width, hidden), BF16),
        pltpu.VMEM((experts * hidden, width), BF16),
        pltpu.VMEM((chunks, rows, width), BF16),
        pltpu.VMEM((chunks, rows, width), BF16),
        pltpu.VMEM((width, tokens), BF16),
        pltpu.VMEM((width, tokens), BF16),
        pltpu.VMEM((width, tokens), BF16),
        pltpu.VMEM((width, tokens), BF16),
        pltpu.VMEM((3, tokens, heads), BF16),
        pltpu.VMEM((micros, PAIRS, LEN, 2 * LEN), F32),
        pltpu.VMEM((tokens, heads), BF16),
        pltpu.VMEM((tokens, width), F32),
        pltpu.VMEM((tokens, hidden), F32),
        pltpu.VMEM((tokens, experts * hidden), BF16),
        pltpu.VMEM((tokens, experts * hidden), BF16),
        pltpu.VMEM((tokens, width), F32),
        pltpu.VMEM((chunks, rows, 1), F32),
        pltpu.VMEM((tokens, 3 * heads), BF16),
        pltpu.VMEM((slots, rows, width), BF16),
        pltpu.VMEM((slots, rows, width), BF16),
        pltpu.VMEM((PAIRS, LEN, 2 * LEN), F32),
        pltpu.VMEM((PAIRS, LEN, 2 * LEN), F32),
        pltpu.SemaphoreType.DMA((5,)),
        pltpu.SemaphoreType.DMA((slots,)),
        pltpu.SemaphoreType.DMA((slots,)),
        pltpu.SemaphoreType.DMA((2 * chunks,)),
        pltpu.SemaphoreType.DMA((2 * chunks,)),
    ]
    return pl.pallas_call(
        kernel,
        out_shape=[
            jax.ShapeDtypeStruct((chunks, rows, width), BF16),
            jax.ShapeDtypeStruct((chunks, rows, width), BF16),
            jax.ShapeDtypeStruct((shards, 2 * width // shards, columns), BF16),
            jax.ShapeDtypeStruct((8, width), F32),
            jax.ShapeDtypeStruct((2 * PAIRS, buckets, LEN), F32),
        ],
        in_specs=[anywhere, anywhere, vmem, vmem, vmem, smem, vmem, vmem] + [anywhere] * 4,
        out_specs=[vmem] * 5,
        scratch_shapes=scratch,
        compiler_params=pltpu.CompilerParams(
            collective_id=0, has_side_effects=True, vmem_limit_bytes=62 * 2**20
        ),
        cost_estimate=pl.CostEstimate(flops=18 * 10**9, bytes_accessed=30 * 10**6, transcendentals=10**6),
    )(
        inputs.reshape(chunks, rows, width),
        cotangent.reshape(chunks, rows, width),
        segments,
        routes.reshape(chunks, rows, 1),
        gain_attn,
        rel_table,
        gain_ffn,
        (router[:, 0] - router[:, 1])[None, :],
        w_qkv,
        w_att_out,
        w_in.reshape(experts * width, hidden),
        w_out.reshape(experts * hidden, width),
    )


def unfolded(shard, columns):
    tiles = columns // (2 * LEN)
    rows = shard.shape[0] // 2
    return shard.reshape(2, rows, tiles, LEN).transpose(1, 2, 0, 3).reshape(rows, columns)


def per_device(
    inputs, cotangent, segments, routes, gain_attn, w_qkv, rel_table, w_att_out, gain_ffn, router, w_in, w_out
):
    experts, width, hidden = w_in.shape[1:]
    heads = w_att_out.shape[1]
    shards = lax.axis_size("dp")
    sec, dgrad, grads, small, tables = local_pass(
        inputs, cotangent, segments, routes[0], gain_attn, w_qkv[0], rel_table[0], w_att_out[0],
        gain_ffn, router[0], w_in[0], w_out[0], shards,
    )
    columns = 2 * grads.shape[2]
    mine = lax.psum_scatter(grads, "dp", scatter_dimension=0, tiled=True)[0].astype(F32)
    mine = unfolded(mine, columns)
    rows = mine.shape[0]
    both = experts * hidden
    g_out = mine[:, :both].reshape(rows, experts, hidden).transpose(1, 2, 0)
    g_in = mine[:, both : 2 * both].reshape(rows, experts, hidden).transpose(1, 0, 2)
    rest = mine[:, 2 * both :]
    g_qkv = rest[:, : 3 * heads].reshape(rows, 3, heads).transpose(1, 0, 2)
    g_att = jnp.concatenate([rest[:, 3 * heads + LEN :], rest[:, 3 * heads : 3 * heads + LEN]], axis=1).T
    flat = jnp.concatenate([small[:3].reshape(-1), tables.sum(axis=2).T.reshape(-1)])
    flat = lax.psum(flat, "dp")
    gain_a, gain_f, routed = flat[:width], flat[width : 2 * width], flat[2 * width : 3 * width]
    table = flat[3 * width :].reshape(rel_table.shape[1:])
    micros, length = inputs.shape[:2]
    return (
        sec.reshape(1, micros, length, width),
        dgrad.reshape(1, micros, length, width),
        gain_a[None],
        g_qkv[None],
        table[None],
        g_att[None],
        gain_f[None],
        jnp.stack([routed, -routed], axis=1)[None],
        g_in[None],
        g_out[None],
    )


def solution(mesh):
    placed = (
        P(None, "dp", None),
        P(None, "dp", None),
        P(None, "dp"),
        P("pipe", None, "dp", None),
        P("pipe", None),
        P("pipe", None, None, "tensor"),
        P("pipe", None, "tensor"),
        P("pipe", "tensor", None),
        P("pipe", None),
        P("pipe", None, None),
        P("pipe", None, None, "tensor"),
        P("pipe", None, "tensor", None),
    )
    return jax.shard_map(
        per_device,
        mesh=mesh,
        in_specs=placed,
        out_specs=(
            P("pipe", None, "dp", None),
            P("pipe", None, "dp", None),
            P("pipe", None),
            P("pipe", None, "dp", "tensor"),
            P("pipe", None, "tensor"),
            P("pipe", "tensor", "dp"),
            P("pipe", None),
            P("pipe", None, None),
            P("pipe", None, "dp", "tensor"),
            P("pipe", None, "tensor", "dp"),
        ),
        check_vma=False,
    )
```

time: 848 us -> 324 us (0.38); the launches traced: 836 us -> 323 us
  matrix products: 222 us -> 0 us
  local copies, waits for them, and re-layouts: 217 us -> 12.7 us
  waiting for transfers between devices: 142 us -> 25.3 us
  Pallas kernels: 0 us -> 107 us
  other arithmetic: 98 us -> 4.02 us
  blocking collectives: 88.1 us -> 160 us
  starting transfers between devices: 50.5 us -> 0.04 us
    dot_general x116 -> x0, matrix products: 222 us -> none  [the longest x5 39.3 us: expert_backward(): jnp.einsum('td,etf->edf', kept['normed2'], d_inner, preferred_element_typ...]
    psum x0 -> x1, blocking collectives: none -> 160 us  [per_device(): flat = lax.psum(flat, 'dp')]
    reshape x7 -> x8, local copies, waits for them, and re-layouts: 112 us -> 3.03 us  [the longest x3 2.37 us: unfolded(): shard.reshape(2, rows, tiles, LEN).transpose(1, 2, 0, 3)]
    pallas_call x0 -> x1, Pallas kernels: none -> 107 us  [local_pass(): pl.pallas_call(kernel, out_shape=[jax.ShapeDtypeStruct((chunks, rows, wid...]
    all_to_all x21 -> x0, blocking collectives: 88.1 us -> none  [copy_for_each(): return lax.all_to_all(copies, axis, split_axis=0, concat_axis=0, tiled=True)]
    reduce_scatter x1, waiting for transfers between devices: 112 us -> 25.3 us  [per_device(): lax.psum_scatter(grads, 'dp', scatter_dimension=0, tiled=True)[0]]
    slice x42 -> x6, local copies, waits for them, and re-layouts: 40.4 us -> 0.06 us  [the longest x1 0.04 us: per_device(): g_out = mine[:, :both].reshape(rows, experts, hidden).transpose(1, 2, 0)]
    reduce_sum x68 -> x1, other arithmetic: 38.6 us -> 0.1 us  [per_device(): tables.sum(axis=2).T.reshape(-1)]
  transfers between devices with their start and end apart: 14 -> 1, of which waited for: 9 -> 1; matrix products, arithmetic and copies ran while one was open for 10% -> 1% of each run, Pallas kernels for 0% -> 0%
where the time goes in v1:
time: 324 us; the launch traced here: 323 us
  blocking collectives  160 us (49%)
  Pallas kernels  107 us (33%)
  waiting for transfers between devices  25.3 us (8%)
  between operations  14.2 us (4%)
  local copies, waits for them, and re-layouts  12.7 us (4%)
  other arithmetic  4.02 us (1%)
    psum x1, blocking collectives, per_device(): flat = lax.psum(flat, 'dp')  160 us
    pallas_call x1, Pallas kernels, local_pass(): pl.pallas_call(kernel, out_shape=[jax.ShapeDtypeStruct((chunks, rows, wid...  107 us
    reduce_scatter x1, waiting for transfers between devices, per_device(): lax.psum_scatter(grads, 'dp', scatter_dimension=0, tiled=True)[0]  25.3 us
    unnamed x16, local copies, waits for them, and re-layouts  7.34 us
  transfers between devices with their start and end apart: 1, of which 1 were waited for; matrix products, arithmetic and copies ran while one was open for 1% of the time, Pallas kernels for 0%

profile of v1, /device:TPU:0, one launch (start us, length us, event | category | flops | bytes accessed | tf_op | source)
XLA Modules:
  0.0 323.2 jit_solution(11510610868811203735)
XLA Ops:
  7.2 0.0 reduce-scatter.2.cloned.1.call-start
  7.2 0.5 broadcast.3
  7.7 1.3 reduce.3
  9.1 0.9 reshape_squeeze.12.routes
  10.0 1.4 copy.38
  11.4 1.3 fusion.rdiff
  12.7 106.8 %shard_map.195 = (bf16[2,256,768]{2,1,0:T(8,128)(2,1)}, bf16[2,256,768]{2,1,0:T(8,128)(2,1)}, bf16[32,48,3840]{2,1,0:T(8,128)(2,1)}, f32[8,768]{1,0:T(8,128)}, f32[6,32,128]{2,1,0:T(8,128)}) custom-call(bf16[2,256,768]{2,1,0:T(8,128)(2,1)} %bitcast.42, bf16[2,256,768]{2,1,0:T(8,128)(2,1)} %bitcast.43, s32[4,128]{1,0:T(4,128)} %segs.1, ...), custom_call_target="tpu_custom_call" | custom-call | flops 17999998976 | bytes 30000000 | tf_op jit(solution)/shard_map/pallas_call | solution.py:415
  119.6 0.0 reduce-scatter.2.cloned.1.call-update
  119.6 0.7 copy-done.3
  120.3 0.2 copy-done.2
  120.5 0.1 reduce_sum.9
  120.6 0.1 copy.40
  120.7 0.1 reshape.88
  120.8 160.1 %psum.7 = f32[2496]{0:T(1024)S(1)} all-reduce(f32[2496]{0:T(1024)S(1)} %pad_maximum_fusion), channel_id=1, replica_groups=mesh['pipe'=2,'dp'=32,'tensor'=2] {'dp'}, use_global_device_ids=true, to_apply=%region_1.0 | all-reduce | flops 2496 | bytes 19968 | tf_op jit(solution)/shard_map/psum | solution.py:474
  280.9 0.6 broadcast_in_dim.22
  281.5 0.6 broadcast_in_dim.25
  282.1 0.1 broadcast_in_dim_reshape.3
  282.2 0.7 copy.43
  282.9 0.6 maximum_bitcast_fusion.1
  283.5 25.3 %reduce-scatter.2.cloned.1.call-done = bf16[1,48,3840]{2,1,0:T(8,128)(2,1)} async-done(((bf16[32,48,3840]{2,1,0:T(8,128)(2,1)}), bf16[1,48,3840]{2,1,0:T(8,128)(2,1)}) %reduce-scatter.2.cloned.1.call-update) | async-done | bytes 368656 | tf_op jit(solution)/shard_map/reduce_scatter | solution.py:464
  308.8 1.2 reshape.98
  310.0 0.0 copy-start
  310.0 0.6 copy.41
  310.6 0.6 reshape.95
  311.2 0.3 reshape.92
  311.5 0.8 copy.44
  312.3 0.3 reshape.93
  312.5 0.8 copy.45
  313.3 0.7 copy.42
  314.0 0.6 maximum_bitcast_fusion
  314.6 0.9 copy.48
  315.5 0.9 copy.49
  (17 shorter events, 0.2 us)
Async XLA Ops:
  7.2 301.6 %reduce-scatter.2.cloned.1.call-start = ((), (), s32[]{:S(2)}) async-start(), calls=%async_computation.1 | async-start | bytes 12165120 | tf_op jit(solution)/shard_map/reduce_scatter | solution.py:464
  119.5 0.7 copy-start.3
  119.6 0.9 copy-start.2
  119.6 195.0 %copy-start.1 = (bf16[2,256,768]{2,1,0:T(8,128)(2,1)S(1)}, bf16[2,256,768]{2,1,0:T(8,128)(2,1)}, u32[]{:S(2)}) copy-start(bf16[2,256,768]{2,1,0:T(8,128)(2,1)} %get-tuple-element.15) | copy-start | bytes 2359300
  310.0 5.5 %copy-start = (bf16[2,256,768]{2,1,0:T(8,128)(2,1)S(1)}, bf16[2,256,768]{2,1,0:T(8,128)(2,1)}, u32[]{:S(2)}) copy-start(bf16[2,256,768]{2,1,0:T(8,128)(2,1)} %get-tuple-element.16) | copy-start | bytes 2359300
Sparse Core Ops, SparseCore 0:
  119.7 188.9 reduce-scatter.1

commit v2 on v1

--- a/solution.py
+++ b/solution.py
@@ -12,6 +12,8 @@
 LEN = 128
 PAIRS = 3
 SEQS = 2
+RING = 4
+STAGES = ((0, 12), (12, 24), (24, 30))
 epsilon = 1e-06
 masked_value = -1e30
 F32 = jnp.float32
@@ -57,10 +59,11 @@
 
 def kernel(
     x_hbm, dy_hbm, segs, routes, gain_a, table, gain_f, rdiff, wqkv_hbm, watt_hbm, win_hbm, wout_hbm,
-    sec, dgrad, grads, small, tables,
+    sec, dgrad, g_out, g_in, g_qkv, g_att, small,
     wqkv, watt, win, wout, hs, dys, xt, nt, rt, at, proj, probs, mixed, after, slope, act2, back2,
-    result, chosens, dproj, send, recv, bias, dsum,
-    load_sem, out_sem, in_sem, pipe_out, pipe_in,
+    result, chosens, dproj, send, recv, bias, dsum, tables, grads, wide0, wide1, wide2, narrow0, narrow1,
+    narrow2, pair0, pair1, pair2, own, lots,
+    load_sem, out_sem, in_sem, pipe_out, pipe_in, ring_out, ring_in, lot_out, lot_in,
 ):
     pipe = lax.axis_index("pipe")
     tensor = lax.axis_index("tensor")
@@ -94,11 +97,23 @@
     barrier = pltpu.get_barrier_semaphore()
     pl.semaphore_signal(barrier, inc=1, device_id={"tensor": 1 - tensor}, device_id_type=pl.DeviceIdType.MESH)
     pl.semaphore_signal(barrier, inc=1, device_id={"pipe": 1 - pipe}, device_id_type=pl.DeviceIdType.MESH)
-    pl.semaphore_wait(barrier, 2)
+    place = lax.axis_index("dp")
+    at_x, at_y, at_z = place // (2 * RING), place // RING % 2, place % RING
+
+    def neighbour(on_x, steps):
+        if on_x:
+            return {"dp": (at_x + steps) % RING * 2 * RING + at_y * RING + at_z}
+        return {"dp": at_x * 2 * RING + at_y * RING + (at_z + steps) % RING}
+
+    across = {"dp": at_x * 2 * RING + (1 - at_y) * RING + at_z}
+    peers = [neighbour(on_x, steps) for on_x in (True, False) for steps in (1, RING - 1)] + [across]
+    for peer in peers:
+        pl.semaphore_signal(barrier, inc=1, device_id=peer, device_id_type=pl.DeviceIdType.MESH)
+    pl.semaphore_wait(barrier, 2 + len(peers))
 
     def to_other_core(slot):
         return pltpu.make_async_remote_copy(
-            src_ref=send.at[slot], dst_ref=recv.at[slot], send_sem=out_sem.at[slot],
+            src_ref=send, dst_ref=recv.at[slot], send_sem=out_sem.at[slot],
             recv_sem=in_sem.at[slot], device_id={"tensor": 1 - tensor},
             device_id_type=pl.DeviceIdType.MESH,
         )
@@ -117,18 +132,19 @@
         return to_other_section(dgrad.at[c], dys.at[c], chunks + c)
 
     def exchanged(slot, part):
-        send[slot] = part.astype(BF16)
+        send[...] = part.astype(BF16)
         copy = to_other_core(slot)
         copy.start()
         copy.wait()
-        return send[slot].astype(F32) + recv[slot].astype(F32)
+        return send[...].astype(F32) + recv[slot].astype(F32)
 
     bucket = bucket_map(buckets)
     lane = lax.broadcasted_iota(jnp.int32, (LEN, LEN), 1)
     upper = lane >= HEAD
     bias[...] = jnp.zeros_like(bias)
     dsum[...] = jnp.zeros_like(dsum)
-    small[...] = jnp.zeros_like(small)
+    own[...] = jnp.zeros_like(own)
+    tables[...] = jnp.zeros_like(tables)
 
     def add_bias(b, carry):
         hit = bucket == b
@@ -153,6 +169,184 @@
         return jnp.concatenate(
             [jnp.broadcast_to(left, (LEN, LEN)), jnp.broadcast_to(right, (LEN, LEN))], axis=1
         )
+
+    def keep(tile, left, right):
+        left, right = [
+            side.reshape(RING, 2, RING, side.shape[0] // (2 * RING * RING), LEN) for side in (left, right)
+        ]
+        both = jnp.concatenate([left, right], axis=3).astype(BF16)
+        grads[:, :, :, :, pl.ds(pl.multiple_of(tile * LEN, LEN), LEN)] = both
+
+    def product_tiles(tile, lefts, rights, count):
+        def one(n, carry):
+            lanes = pl.ds(pl.multiple_of(n * 2 * LEN, 2 * LEN), 2 * LEN)
+            made = dot(lefts[...], rights[:, lanes])
+            keep(tile + n, made[:, :LEN], made[:, LEN:])
+            return carry
+
+        lax.fori_loop(0, count, one, 0)
+
+    out_tiles = 2 * hidden // (2 * LEN)
+    wides, narrows, doubles = (wide0, wide1, wide2), (narrow0, narrow1, narrow2), (pair0, pair1, pair2)
+
+    def lanes_of(stage, part):
+        begin, end = STAGES[stage]
+        count = (end - begin) // 2
+        return begin + part * count, count
+
+    class Ring:
+        def __init__(self, stage, part, phase):
+            begin, count = lanes_of(stage, part)
+            self.lanes = pl.ds(begin * LEN, count * LEN)
+            self.part, self.phase = part, phase
+            on_x = (part == 0) == (phase == 0)
+            self.me = at_x if on_x else at_z
+            self.up, self.down, self.far = [(self.me + steps) % RING for steps in (1, 3, 2)]
+            self.landing = (wides, narrows)[phase][stage].at[part]
+            base = ((stage * 2 + part) * 2 + phase) * 6
+            plan = ((self.far, 0, 1), (self.far, 1, 3), (self.up, 1, 1), (self.down, 0, 3), (self.up, 0, 1), (self.down, 1, 3))
+            slots = (0, 1, 3, 4, 2, 5)
+            self.copies = [
+                pltpu.make_async_remote_copy(
+                    src_ref=self.block(whose, half), dst_ref=self.landing.at[slot], send_sem=ring_out.at[base + i],
+                    recv_sem=ring_in.at[base + i], device_id=neighbour(on_x, steps),
+                    device_id_type=pl.DeviceIdType.MESH,
+                )
+                for i, ((whose, half, steps), slot) in enumerate(zip(plan, slots))
+            ]
+
+        def block(self, whose, half):
+            if self.phase == 0:
+                if self.part == 0:
+                    return grads.at[whose, half, :, :, self.lanes]
+                return grads.at[:, half, whose, :, self.lanes]
+            if self.part == 0:
+                return grads.at[at_x, half, whose, :, self.lanes]
+            return grads.at[whose, half, at_z, :, self.lanes]
+
+        def pieces(self, refs):
+            return [[ref.at[i] for ref in refs] for i in range(RING)] if self.phase == 0 else [refs]
+
+        def add(self, *refs):
+            for target, *others in self.pieces(refs):
+                total = target[...].astype(F32)
+                for other in others:
+                    total = total + other[...].astype(F32)
+                target[...] = total.astype(BF16)
+
+        def begin(self):
+            for copy in self.copies[:4]:
+                copy.start()
+
+        def relay(self):
+            self.copies[0].wait_recv()
+            self.add(self.block(self.up, 0), self.landing.at[0])
+            self.copies[4].start()
+            self.copies[1].wait_recv()
+            self.add(self.block(self.down, 1), self.landing.at[1])
+            self.copies[5].start()
+
+        def close(self):
+            for copy in self.copies[2:]:
+                copy.wait_recv()
+            for half in range(2):
+                self.add(self.block(self.me, half), self.landing.at[2 + half], self.landing.at[4 + half])
+
+        def drain(self):
+            for copy in self.copies:
+                copy.wait_send()
+
+    rings = [[[Ring(stage, part, phase) for part in range(2)] for phase in range(2)] for stage in range(len(STAGES))]
+
+    def swap(stage, part):
+        begin, count = lanes_of(stage, part)
+        slot = len(STAGES) * 24 + stage * 2 + part
+        return pltpu.make_async_remote_copy(
+            src_ref=grads.at[at_x, 1 - at_y, at_z, :, pl.ds(begin * LEN, count * LEN)],
+            dst_ref=doubles[stage].at[part], send_sem=ring_out.at[slot], recv_sem=ring_in.at[slot],
+            device_id=across, device_id_type=pl.DeviceIdType.MESH,
+        )
+
+    def begin(stage, phase):
+        for ring in rings[stage][phase]:
+            ring.begin()
+
+    def relay(stage, phase):
+        for ring in rings[stage][phase]:
+            ring.relay()
+
+    def close(stage, phase):
+        for part, ring in enumerate(rings[stage][phase]):
+            ring.close()
+            if phase == 0:
+                rings[stage][1][part].begin()
+            else:
+                swap(stage, part).start()
+
+    def place_tile(tile, top, bottom):
+        pair = pl.ds(tile % out_tiles * 2 * LEN, 2 * LEN)
+        if tile < out_tiles:
+            g_out[:, pair] = jnp.concatenate([top, bottom], axis=1)
+        elif tile < 2 * out_tiles:
+            within = (tile - out_tiles) * 2 * LEN
+            g_in[within // hidden, :, pl.ds(within % hidden, 2 * LEN)] = jnp.concatenate([top, bottom], axis=1)
+        elif tile < 2 * out_tiles + 5:
+            at_block = 2 * (tile - 2 * out_tiles)
+            g_qkv[at_block // PAIRS, :, pl.ds(at_block % PAIRS * LEN, LEN)] = top
+            if tile < 2 * out_tiles + 4:
+                g_qkv[(at_block + 1) // PAIRS, :, pl.ds((at_block + 1) % PAIRS * LEN, LEN)] = bottom
+            else:
+                g_att[:, 2 * LEN :] = bottom
+        else:
+            g_att[:, : 2 * LEN] = jnp.concatenate([top, bottom], axis=1)
+
+    def settle(stage):
+        for part in range(2):
+            swap(stage, part).wait_recv()
+            begin_tile, count = lanes_of(stage, part)
+            lanes = pl.ds(begin_tile * LEN, count * LEN)
+            total = grads[at_x, at_y, at_z, :, lanes].astype(F32) + doubles[stage][part].astype(F32)
+            half = total.shape[0] // 2
+            for i in range(count):
+                here = slice(i * LEN, (i + 1) * LEN)
+                place_tile(begin_tile + i, total[:half, here], total[half:, here])
+
+    def lot(slot, source, target, peer):
+        return pltpu.make_async_remote_copy(
+            src_ref=source, dst_ref=lots.at[target], send_sem=lot_out.at[slot], recv_sem=lot_in.at[slot],
+            device_id=peer, device_id_type=pl.DeviceIdType.MESH,
+        )
+
+    lot_copies = []
+    for phase in range(2):
+        up, down = neighbour(phase == 0, 1), neighbour(phase == 0, RING - 1)
+        base = 4 * phase
+        lot_copies += [
+            lot(3 * phase, own.at[phase], base, up),
+            lot(3 * phase + 1, own.at[phase], base + 1, down),
+            lot(3 * phase + 2, lots.at[base], base + 2, up),
+        ]
+    lot_copies.append(lot(6, own.at[2], 8, across))
+
+    def lots_open(phase):
+        lot_copies[3 * phase].start()
+        lot_copies[3 * phase + 1].start()
+
+    def lots_pass(phase):
+        lot_copies[3 * phase].wait_recv()
+        lot_copies[3 * phase + 2].start()
+
+    def lots_sum(phase):
+        lot_copies[3 * phase + 1].wait_recv()
+        lot_copies[3 * phase + 2].wait_recv()
+        base = 4 * phase
+        own[phase + 1] = (own[phase] + lots[base + 2]) + (lots[base] + lots[base + 1])
+
+    def expert_gradients():
+        product_tiles(0, rt, act2, out_tiles)
+        begin(0, 0)
+        product_tiles(out_tiles, nt, back2, out_tiles)
+        begin(1, 0)
 
     for load in loads:
         load.wait()
@@ -210,9 +404,10 @@
             squared = inner * inner
             root = np.sqrt(2 / np.pi).astype(np.float32)
             bend = jnp.tanh(root * inner * (1.0 + 0.044715 * squared))
-            slope[here, lanes] = 0.5 * (1.0 + bend) + 0.5 * inner * (1.0 - bend * bend) * root * (
+            steep = 0.5 * (1.0 + bend) + 0.5 * inner * (1.0 - bend * bend) * root * (
                 1.0 + 3 * 0.044715 * squared
             )
+            slope[here, lanes] = steep.astype(BF16)
             active = (0.5 * inner * (1.0 + bend)).astype(BF16)
             act2[here, lanes] = active * to_zero
             act2[here, pl.ds(pl.multiple_of(hidden + n * step, step), step)] = active * to_one
@@ -220,7 +415,7 @@
 
         lax.fori_loop(0, hidden // step, inner_tile, 0)
         total = exchanged(4 * c + 1, dot(act2[here, :], wout[...]))
-        result[here, :] = total
+        result[here, :] = total.astype(BF16)
         sec[c] = (after[here, :] + chosen * total).astype(BF16)
 
         @pl.when(first)
@@ -248,7 +443,7 @@
         to_zero = (route == 0).astype(BF16)
         to_one = (route == 1).astype(BF16)
         chosen = chosens[c]
-        d_logit = sign * over_lanes(dy * result[here, :]) * chosen * (1.0 - chosen)
+        d_logit = sign * over_lanes(dy * result[here, :].astype(F32)) * chosen * (1.0 - chosen)
         d_result = (chosen * dy).astype(BF16)
         rt[:, here] = d_result.T
         zero_part = d_result * to_zero
@@ -260,12 +455,17 @@
             d_active = dot(zero_part, wout[pl.ds(low, step), :], NT) + dot(
                 one_part, wout[pl.ds(high, step), :], NT
             )
-            d_inner = (d_active * slope[here, pl.ds(low, step)]).astype(BF16)
+            d_inner = (d_active * slope[here, pl.ds(low, step)].astype(F32)).astype(BF16)
             back2[here, pl.ds(low, step)] = d_inner * to_zero
             back2[here, pl.ds(high, step)] = d_inner * to_one
             return carry
 
         lax.fori_loop(0, hidden // step, active_tile, 0)
+
+        @pl.when(first & (c == chunks - 1))
+        def _():
+            expert_gradients()
+
         d_normed2 = dot(back2[here, :hidden], win[:width, :], NT) + dot(
             back2[here, hidden:], win[width:, :], NT
         )
@@ -274,8 +474,8 @@
         scale = lax.rsqrt(jnp.mean(a * a, axis=1, keepdims=True) + epsilon)
         plain = a * scale
         normed2 = (plain * gain_f[...]).astype(BF16).astype(F32)
-        small[1:2, :] += over_rows(d_normed2 * plain)
-        small[2:3, :] += over_rows(normed2 * d_logit)
+        own[0, 1:2, :] += over_rows(d_normed2 * plain)
+        own[0, 2:3, :] += over_rows(normed2 * d_logit)
         pulled = d_normed2 * gain_f[...]
         d_after = dy + scale * (pulled - plain * jnp.mean(pulled * plain, axis=1, keepdims=True))
         after[here, :] = d_after
@@ -307,7 +507,7 @@
         h = hs[c].astype(F32)
         scale = lax.rsqrt(jnp.mean(h * h, axis=1, keepdims=True) + epsilon)
         plain = h * scale
-        small[0:1, :] += over_rows(d_normed * plain)
+        own[0, 0:1, :] += over_rows(d_normed * plain)
         pulled = d_normed * gain_a[...]
         d_hidden = after[here, :] + scale * (
             pulled - plain * jnp.mean(pulled * plain, axis=1, keepdims=True)
@@ -322,37 +522,56 @@
 
     lax.fori_loop(0, chunks, backward, 0)
 
-    def keep(tile, left, right):
-        shards, double, _ = grads.shape
-        both = [side.reshape(shards, double // 2, LEN) for side in (left, right)]
-        grads[:, :, pl.ds(pl.multiple_of(tile * LEN, LEN), LEN)] = jnp.concatenate(both, axis=1).astype(BF16)
-
-    def product_tiles(tile, lefts, rights, count):
-        def one(n, carry):
-            lanes = pl.ds(pl.multiple_of(n * 2 * LEN, 2 * LEN), 2 * LEN)
-            made = dot(lefts[...], rights[:, lanes])
-            keep(tile + n, made[:, :LEN], made[:, LEN:])
-            return carry
-
-        lax.fori_loop(0, count, one, 0)
-
-    out_tiles = 2 * hidden // (2 * LEN)
-    product_tiles(0, rt, act2, out_tiles)
-    product_tiles(out_tiles, nt, back2, out_tiles)
-    product_tiles(2 * out_tiles, xt, dproj, 4)
-    keep(2 * out_tiles + 4, dot(xt[...], dproj[:, 8 * LEN :]), dot(at[...], mixed[:, 2 * LEN :]))
-    made = dot(at[...], mixed[:, : 2 * LEN])
-    keep(2 * out_tiles + 5, made[:, :LEN], made[:, LEN:])
+    @pl.when(last)
+    def _():
+        expert_gradients()
 
     def table_rows(b, carry):
         hit = bucket == b
         for pair in range(PAIRS):
             for side in range(2):
                 picked = jnp.where(hit, dsum[pair, :, pl.ds(side * LEN, LEN)], 0.0)
-                tables[2 * pair + side, pl.ds(b, 1), :] = over_rows(picked)
+                tables[pl.ds((2 * pair + side) * buckets + b, 1), :] = over_rows(picked)
         return carry
 
     lax.fori_loop(0, buckets, table_rows, 0)
+    own[0, 3:4, : 2 * LEN] = over_rows(tables[...].T)
+    lots_open(0)
+    relay(0, 0)
+    product_tiles(2 * out_tiles, xt, dproj, 4)
+    keep(2 * out_tiles + 4, dot(xt[...], dproj[:, 8 * LEN :]), dot(at[...], mixed[:, 2 * LEN :]))
+    made = dot(at[...], mixed[:, : 2 * LEN])
+    keep(2 * out_tiles + 5, made[:, :LEN], made[:, LEN:])
+    begin(2, 0)
+    lots_pass(0)
+    relay(1, 0)
+    lots_sum(0)
+    lots_open(1)
+    close(0, 0)
+    lots_pass(1)
+    relay(2, 0)
+    lots_sum(1)
+    lot_copies[6].start()
+    relay(0, 1)
+    close(1, 0)
+    close(0, 1)
+    relay(1, 1)
+    close(2, 0)
+    settle(0)
+    close(1, 1)
+    relay(2, 1)
+    settle(1)
+    lot_copies[6].wait_recv()
+    small[...] = own[2] + lots[8]
+    close(2, 1)
+    settle(2)
+    for copy in lot_copies:
+        copy.wait_send()
+    for stage in range(len(STAGES)):
+        for part in range(2):
+            rings[stage][0][part].drain()
+            rings[stage][1][part].drain()
+            swap(stage, part).wait_send()
 
     def finish(c, carry):
         @pl.when(first)
@@ -368,7 +587,7 @@
     lax.fori_loop(0, chunks, finish, 0)
 
 
-def local_pass(inputs, cotangent, segments, routes, gain_attn, w_qkv, rel_table, w_att_out, gain_ffn, router, w_in, w_out, shards):
+def local_pass(inputs, cotangent, segments, routes, gain_attn, w_qkv, rel_table, w_att_out, gain_ffn, router, w_in, w_out):
     micros, length, width = inputs.shape
     chunks = micros // SEQS
     rows = SEQS * length
@@ -381,6 +600,9 @@
     smem = pl.BlockSpec(memory_space=pltpu.SMEM)
     anywhere = pl.BlockSpec(memory_space=pl.ANY)
     slots = 4 * chunks
+    shard = width // (2 * RING * RING)
+    double = 2 * shard
+    pieces = [(end - begin) // 2 * LEN for begin, end in STAGES]
     scratch = [
         pltpu.VMEM(w_qkv.shape, BF16),
         pltpu.VMEM(w_att_out.shape, BF16),
@@ -396,33 +618,46 @@
         pltpu.VMEM((micros, PAIRS, LEN, 2 * LEN), F32),
         pltpu.VMEM((tokens, heads), BF16),
         pltpu.VMEM((tokens, width), F32),
-        pltpu.VMEM((tokens, hidden), F32),
+        pltpu.VMEM((tokens, hidden), BF16),
         pltpu.VMEM((tokens, experts * hidden), BF16),
         pltpu.VMEM((tokens, experts * hidden), BF16),
-        pltpu.VMEM((tokens, width), F32),
+        pltpu.VMEM((tokens, width), BF16),
         pltpu.VMEM((chunks, rows, 1), F32),
         pltpu.VMEM((tokens, 3 * heads), BF16),
-        pltpu.VMEM((slots, rows, width), BF16),
+        pltpu.VMEM((rows, width), BF16),
         pltpu.VMEM((slots, rows, width), BF16),
         pltpu.VMEM((PAIRS, LEN, 2 * LEN), F32),
         pltpu.VMEM((PAIRS, LEN, 2 * LEN), F32),
+        pltpu.VMEM((2 * LEN, LEN), F32),
+        pltpu.VMEM((RING, 2, RING, double, columns), BF16),
+        *[pltpu.VMEM((2, 6, RING, double, piece), BF16) for piece in pieces],
+        *[pltpu.VMEM((2, 6, double, piece), BF16) for piece in pieces],
+        *[pltpu.VMEM((2, double, piece), BF16) for piece in pieces],
+        pltpu.VMEM((3, 8, width), F32),
+        pltpu.VMEM((9, 8, width), F32),
         pltpu.SemaphoreType.DMA((5,)),
         pltpu.SemaphoreType.DMA((slots,)),
         pltpu.SemaphoreType.DMA((slots,)),
         pltpu.SemaphoreType.DMA((2 * chunks,)),
         pltpu.SemaphoreType.DMA((2 * chunks,)),
+        pltpu.SemaphoreType.DMA((26 * len(STAGES),)),
+        pltpu.SemaphoreType.DMA((26 * len(STAGES),)),
+        pltpu.SemaphoreType.DMA((7,)),
+        pltpu.SemaphoreType.DMA((7,)),
     ]
     return pl.pallas_call(
         kernel,
         out_shape=[
             jax.ShapeDtypeStruct((chunks, rows, width), BF16),
             jax.ShapeDtypeStruct((chunks, rows, width), BF16),
-            jax.ShapeDtypeStruct((shards, 2 * width // shards, columns), BF16),
+            jax.ShapeDtypeStruct((shard, experts * hidden), F32),
+            jax.ShapeDtypeStruct((experts, shard, hidden), F32),
+            jax.ShapeDtypeStruct((3, shard, heads), F32),
+            jax.ShapeDtypeStruct((shard, heads), F32),
             jax.ShapeDtypeStruct((8, width), F32),
-            jax.ShapeDtypeStruct((2 * PAIRS, buckets, LEN), F32),
         ],
         in_specs=[anywhere, anywhere, vmem, vmem, vmem, smem, vmem, vmem] + [anywhere] * 4,
-        out_specs=[vmem] * 5,
+        out_specs=[vmem] * 7,
         scratch_shapes=scratch,
         compiler_params=pltpu.CompilerParams(
             collective_id=0, has_side_effects=True, vmem_limit_bytes=62 * 2**20
@@ -444,36 +679,18 @@
     )
 
 
-def unfolded(shard, columns):
-    tiles = columns // (2 * LEN)
-    rows = shard.shape[0] // 2
-    return shard.reshape(2, rows, tiles, LEN).transpose(1, 2, 0, 3).reshape(rows, columns)
-
-
 def per_device(
     inputs, cotangent, segments, routes, gain_attn, w_qkv, rel_table, w_att_out, gain_ffn, router, w_in, w_out
 ):
     experts, width, hidden = w_in.shape[1:]
-    heads = w_att_out.shape[1]
-    shards = lax.axis_size("dp")
-    sec, dgrad, grads, small, tables = local_pass(
+    sec, dgrad, g_out, g_in, g_qkv, g_att, small = local_pass(
         inputs, cotangent, segments, routes[0], gain_attn, w_qkv[0], rel_table[0], w_att_out[0],
-        gain_ffn, router[0], w_in[0], w_out[0], shards,
+        gain_ffn, router[0], w_in[0], w_out[0],
     )
-    columns = 2 * grads.shape[2]
-    mine = lax.psum_scatter(grads, "dp", scatter_dimension=0, tiled=True)[0].astype(F32)
-    mine = unfolded(mine, columns)
-    rows = mine.shape[0]
-    both = experts * hidden
-    g_out = mine[:, :both].reshape(rows, experts, hidden).transpose(1, 2, 0)
-    g_in = mine[:, both : 2 * both].reshape(rows, experts, hidden).transpose(1, 0, 2)
-    rest = mine[:, 2 * both :]
-    g_qkv = rest[:, : 3 * heads].reshape(rows, 3, heads).transpose(1, 0, 2)
-    g_att = jnp.concatenate([rest[:, 3 * heads + LEN :], rest[:, 3 * heads : 3 * heads + LEN]], axis=1).T
-    flat = jnp.concatenate([small[:3].reshape(-1), tables.sum(axis=2).T.reshape(-1)])
-    flat = lax.psum(flat, "dp")
-    gain_a, gain_f, routed = flat[:width], flat[width : 2 * width], flat[2 * width : 3 * width]
-    table = flat[3 * width :].reshape(rel_table.shape[1:])
+    buckets, heads = rel_table.shape[1:]
+    g_out = g_out.reshape(-1, experts, hidden).transpose(1, 2, 0)
+    gain_a, gain_f, routed = small[0], small[1], small[2]
+    table = small[3, : buckets * heads].reshape(heads, buckets).T
     micros, length = inputs.shape[:2]
     return (
         sec.reshape(1, micros, length, width),
@@ -481,7 +698,7 @@
         gain_a[None],
         g_qkv[None],
         table[None],
-        g_att[None],
+        g_att.T[None],
         gain_f[None],
         jnp.stack([routed, -routed], axis=1)[None],
         g_in[None],

time: 324 us -> 183 us (0.56)
  blocking collectives: 160 us -> 0 us
  Pallas kernels: 107 us -> 161 us
  waiting for transfers between devices: 25.3 us -> 0 us
  between operations: 14.2 us -> 0.66 us
  local copies, waits for them, and re-layouts: 12.7 us -> 16.1 us
    psum x1 -> x0, blocking collectives: 160 us -> none  [per_device(): flat = lax.psum(flat, 'dp')]
    pallas_call x1, Pallas kernels: 107 us -> 161 us  [local_pass(): pl.pallas_call(kernel, out_shape=[jax.ShapeDtypeStruct((chunks, rows, wid...]
    reduce_scatter x1 -> x0, waiting for transfers between devices: 25.3 us -> none  [per_device(): lax.psum_scatter(grads, 'dp', scatter_dimension=0, tiled=True)[0]]
    unnamed x16 -> x7, local copies, waits for them, and re-layouts: 7.34 us -> 10.6 us
  transfers between devices with their start and end apart: 1 -> 0, of which waited for: 1 -> 0; matrix products, arithmetic and copies ran while one was open for 1% -> 0% of each run, Pallas kernels for 0% -> 0%
where the time goes in v2:
time: 183 us; the launch traced here: 182 us
  Pallas kernels  161 us (88%)
  local copies, waits for them, and re-layouts  16.1 us (9%)
  other arithmetic  4.04 us (2%)
    pallas_call x1, Pallas kernels, local_pass(): pl.pallas_call(kernel, out_shape=[jax.ShapeDtypeStruct((chunks, rows, wid...  161 us
    unnamed x7, local copies, waits for them, and re-layouts  10.6 us

profile of v2, /device:TPU:0, one launch (start us, length us, event | category | flops | bytes accessed | tf_op | source)
XLA Modules:
  0.0 181.9 jit_solution(9240740837109033147)
XLA Ops:
  0.6 0.5 broadcast.6
  1.2 1.3 reduce.7
  2.5 0.9 reshape_squeeze.16.routes
  3.4 1.4 copy.24
  4.8 1.3 fusion.rdiff
  6.1 161.2 %shard_map.195 = (bf16[2,256,768]{2,1,0:T(8,128)(2,1)}, bf16[2,256,768]{2,1,0:T(8,128)(2,1)}, f32[24,3072]{1,0:T(8,128)}, f32[2,24,1536]{2,1,0:T(8,128)}, f32[3,...) custom-call(bf16[2,256,768]{2,1,0:T(8,128)(2,1)} %bitcast.49, bf16[2,256,768]{2,1,0:T(8,128)(2,1)} %bitcast.50, ...), custom_call_target="tpu_custom_call" | custom-call | flops 17999998976 | bytes 30000000 | tf_op jit(solution)/shard_map/pallas_call | solution.py:648
  167.3 1.4 slice_bitcast_fusion
  168.7 0.7 fusion.1
  169.5 0.6 maximum_bitcast_fusion
  170.1 0.7 slice_reduce_fusion
  170.8 0.1 reshape_squeeze.15
  170.9 0.6 broadcast_in_dim.20
  171.5 1.7 copy.29
  173.2 2.1 %copy.35 = bf16[1,4,128,768]{3,2,1,0:T(8,128)(2,1)} copy(bf16[1,4,128,768]{3,2,1,0:T(8,128)(2,1)} %bitcast.37) | data formatting | bytes 1572864
  175.2 2.1 %copy.36 = bf16[1,4,128,768]{3,2,1,0:T(8,128)(2,1)} copy(bf16[1,4,128,768]{3,2,1,0:T(8,128)(2,1)} %bitcast.36) | data formatting | bytes 1572864
  177.3 1.5 copy.37
  178.8 1.4 copy.38
  180.2 1.7 copy.39

commit v3 on v2

--- a/solution.py
+++ b/solution.py
@@ -13,7 +13,13 @@
 PAIRS = 3
 SEQS = 2
 RING = 4
-STAGES = ((0, 12), (12, 24), (24, 30))
+PLAN = (
+    ((0, 0, 4), (1, 4, 4), (2, 8, 2), (3, 10, 2)),
+    ((0, 12, 4), (1, 16, 4), (2, 20, 2), (3, 22, 2)),
+    ((0, 24, 3), (1, 27, 3)),
+)
+PIECES = [piece for stage in PLAN for piece in stage]
+CUTS = 2
 epsilon = 1e-06
 masked_value = -1e30
 F32 = jnp.float32
@@ -58,12 +64,12 @@
 
 
 def kernel(
-    x_hbm, dy_hbm, segs, routes, gain_a, table, gain_f, rdiff, wqkv_hbm, watt_hbm, win_hbm, wout_hbm,
-    sec, dgrad, g_out, g_in, g_qkv, g_att, small,
-    wqkv, watt, win, wout, hs, dys, xt, nt, rt, at, proj, probs, mixed, after, slope, act2, back2,
-    result, chosens, dproj, send, recv, bias, dsum, tables, grads, wide0, wide1, wide2, narrow0, narrow1,
-    narrow2, pair0, pair1, pair2, own, lots,
-    load_sem, out_sem, in_sem, pipe_out, pipe_in, ring_out, ring_in, lot_out, lot_in,
+    x_hbm, dy_hbm, segs_hbm, routes_hbm, gain_a, table, gain_f, router, wqkv_hbm, watt_hbm, win_hbm, wout_hbm,
+    sec_hbm, dgrad_hbm, g_out, g_in, g_qkv, g_att, g_gain_a, g_gain_f, g_router, g_table,
+    segs, routes, signs, sec, dgrad, wqkv, watt, win, wout, hs, dys, xt, nt, rt, at, proj, probs, mixed, after,
+    slope, act2, back2, result, chosens, dproj, send, recv, bias, dsum, tables, grads, own, lots,
+    load_sem, out_sem, in_sem, pipe_out, pipe_in, half_out, half_in, far_out, far_in, ring_out, ring_in,
+    lot_out, lot_in, *landings,
 ):
     pipe = lax.axis_index("pipe")
     tensor = lax.axis_index("tensor")
@@ -72,7 +78,7 @@
     chunks, rows, width = hs.shape
     hidden = slope.shape[-1]
     step = 512
-    buckets = table.shape[0]
+    buckets = table.shape[-1]
 
     loads = [
         pltpu.make_async_copy(source, target, load_sem.at[i])
@@ -80,23 +86,21 @@
             ((wqkv_hbm, wqkv), (watt_hbm, watt), (win_hbm, win), (wout_hbm, wout))
         )
     ]
-    load_x = pltpu.make_async_copy(x_hbm, hs, load_sem.at[4])
-    load_dy = pltpu.make_async_copy(dy_hbm, dys, load_sem.at[4])
+    loads_first = [
+        pltpu.make_async_copy(source, target, load_sem.at[4 + i])
+        for i, (source, target) in enumerate(((x_hbm, hs), (segs_hbm, segs), (routes_hbm, routes)))
+    ]
 
     @pl.when(first)
     def _():
-        load_x.start()
-
-    @pl.when(last)
-    def _():
-        load_dy.start()
+        for load in loads_first:
+            load.start()
 
     for load in loads:
         load.start()
 
     barrier = pltpu.get_barrier_semaphore()
     pl.semaphore_signal(barrier, inc=1, device_id={"tensor": 1 - tensor}, device_id_type=pl.DeviceIdType.MESH)
-    pl.semaphore_signal(barrier, inc=1, device_id={"pipe": 1 - pipe}, device_id_type=pl.DeviceIdType.MESH)
     place = lax.axis_index("dp")
     at_x, at_y, at_z = place // (2 * RING), place // RING % 2, place % RING
 
@@ -106,30 +110,87 @@
         return {"dp": at_x * 2 * RING + at_y * RING + (at_z + steps) % RING}
 
     across = {"dp": at_x * 2 * RING + (1 - at_y) * RING + at_z}
-    peers = [neighbour(on_x, steps) for on_x in (True, False) for steps in (1, RING - 1)] + [across]
+    next_section = {"pipe": 1 - pipe, **across}
+    peers = [next_section] + [neighbour(on_x, steps) for on_x in (True, False) for steps in (1, RING - 1)] + [across]
+
+    def remote(source, target, out, into, device):
+        return pltpu.make_async_remote_copy(
+            src_ref=source, dst_ref=target, send_sem=out, recv_sem=into, device_id=device,
+            device_id_type=pl.DeviceIdType.MESH,
+        )
+
     for peer in peers:
         pl.semaphore_signal(barrier, inc=1, device_id=peer, device_id_type=pl.DeviceIdType.MESH)
-    pl.semaphore_wait(barrier, 2 + len(peers))
+    pl.semaphore_wait(barrier, 1 + len(peers))
+
+    other_core = {"tensor": 1 - tensor}
+    loads_last = [
+        remote(source, target, far_out.at[i], far_in.at[i], across)
+        for i, (source, target) in enumerate(((segs_hbm, segs), (routes_hbm, routes), (dy_hbm, dys)))
+    ]
+
+    @pl.when(last)
+    def _():
+        for load in loads_last:
+            load.start()
 
     def to_other_core(slot):
-        return pltpu.make_async_remote_copy(
-            src_ref=send, dst_ref=recv.at[slot], send_sem=out_sem.at[slot],
-            recv_sem=in_sem.at[slot], device_id={"tensor": 1 - tensor},
-            device_id_type=pl.DeviceIdType.MESH,
-        )
-
-    def to_other_section(source, target, slot):
-        return pltpu.make_async_remote_copy(
-            src_ref=source, dst_ref=target, send_sem=pipe_out.at[slot],
-            recv_sem=pipe_in.at[slot], device_id={"pipe": 1 - pipe},
-            device_id_type=pl.DeviceIdType.MESH,
-        )
+        return remote(send, recv.at[slot], out_sem.at[slot], in_sem.at[slot], other_core)
+
+    def crossing(source, target, c, back):
+        length = rows // (2 * CUTS)
+        sends, shares = [], []
+        for i in range(CUTS):
+            here = pl.ds(pl.multiple_of((tensor * CUTS + i) * length, length), length)
+            slot = (back * chunks + c) * CUTS + i
+            sends.append(
+                remote(source.at[c, here], target.at[c, here], pipe_out.at[slot], pipe_in.at[slot], next_section)
+            )
+            shares.append(
+                remote(target.at[c, here], target.at[c, here], half_out.at[slot], half_in.at[slot], other_core)
+            )
+        return sends, shares
+
+    def cross(crossed):
+        for copy in crossed[0]:
+            copy.start()
+
+    def land(crossed):
+        for arrived, share in zip(*crossed):
+            arrived.wait_recv()
+            share.start()
+        for share in crossed[1]:
+            share.wait_recv()
 
     def forward_copy(c):
-        return to_other_section(sec.at[c], hs.at[c], c)
+        return crossing(sec, hs, c, 0)
 
     def backward_copy(c):
-        return to_other_section(dgrad.at[c], dys.at[c], chunks + c)
+        return crossing(dgrad, dys, c, 1)
+
+    def give(source, target, c, back):
+        slot = back * chunks + c
+        stays = pltpu.make_async_copy(source.at[c], target.at[c], load_sem.at[7 + slot])
+        leaves = remote(source.at[c], target.at[c], far_out.at[3 + slot], far_in.at[3 + slot], across)
+        return stays, leaves
+
+    def give_start(given):
+        @pl.when(first)
+        def _():
+            given[0].start()
+
+        @pl.when(last)
+        def _():
+            given[1].start()
+
+    def give_wait(given):
+        @pl.when(first)
+        def _():
+            given[0].wait()
+
+        @pl.when(last)
+        def _():
+            given[1].wait()
 
     def exchanged(slot, part):
         send[...] = part.astype(BF16)
@@ -151,7 +212,7 @@
         for pair in range(PAIRS):
             for side in range(2):
                 at_lanes = pl.ds(side * LEN, LEN)
-                bias[pair, :, at_lanes] = jnp.where(hit, table[b, 2 * pair + side], bias[pair, :, at_lanes])
+                bias[pair, :, at_lanes] = jnp.where(hit, table[2 * pair + side, 0, b], bias[pair, :, at_lanes])
         return carry
 
     lax.fori_loop(0, buckets, add_bias, 0)
@@ -187,52 +248,51 @@
         lax.fori_loop(0, count, one, 0)
 
     out_tiles = 2 * hidden // (2 * LEN)
-    wides, narrows, doubles = (wide0, wide1, wide2), (narrow0, narrow1, narrow2), (pair0, pair1, pair2)
-
-    def lanes_of(stage, part):
-        begin, end = STAGES[stage]
-        count = (end - begin) // 2
-        return begin + part * count, count
-
     class Ring:
-        def __init__(self, stage, part, phase):
-            begin, count = lanes_of(stage, part)
+        def __init__(self, index, phase):
+            kind, begin, count = PIECES[index]
             self.lanes = pl.ds(begin * LEN, count * LEN)
-            self.part, self.phase = part, phase
-            on_x = (part == 0) == (phase == 0)
+            self.fine = [pl.ds((begin + i * (count // 2)) * LEN, count // 2 * LEN) for i in range(2)]
+            self.kind, self.phase = kind, phase
+            on_x = (kind % 2 == 0) == (phase == 0)
             self.me = at_x if on_x else at_z
             self.up, self.down, self.far = [(self.me + steps) % RING for steps in (1, 3, 2)]
-            self.landing = (wides, narrows)[phase][stage].at[part]
-            base = ((stage * 2 + part) * 2 + phase) * 6
+            self.landing = landings[3 * index + phase]
+            base = index * 13 + phase * 6
             plan = ((self.far, 0, 1), (self.far, 1, 3), (self.up, 1, 1), (self.down, 0, 3), (self.up, 0, 1), (self.down, 1, 3))
             slots = (0, 1, 3, 4, 2, 5)
             self.copies = [
-                pltpu.make_async_remote_copy(
-                    src_ref=self.block(whose, half), dst_ref=self.landing.at[slot], send_sem=ring_out.at[base + i],
-                    recv_sem=ring_in.at[base + i], device_id=neighbour(on_x, steps),
-                    device_id_type=pl.DeviceIdType.MESH,
+                remote(
+                    self.block(whose, half), self.landing.at[slot], ring_out.at[base + i], ring_in.at[base + i],
+                    neighbour(on_x, steps),
                 )
                 for i, ((whose, half, steps), slot) in enumerate(zip(plan, slots))
             ]
 
         def block(self, whose, half):
             if self.phase == 0:
-                if self.part == 0:
+                two = pl.ds(2 * half, 2)
+                if self.kind == 0:
                     return grads.at[whose, half, :, :, self.lanes]
-                return grads.at[:, half, whose, :, self.lanes]
-            if self.part == 0:
+                if self.kind == 1:
+                    return grads.at[:, half, whose, :, self.lanes]
+                if self.kind == 2:
+                    return grads.at[whose, at_y, two, :, self.lanes]
+                return grads.at[two, at_y, whose, :, self.lanes]
+            if self.kind == 0:
                 return grads.at[at_x, half, whose, :, self.lanes]
-            return grads.at[whose, half, at_z, :, self.lanes]
-
-        def pieces(self, refs):
-            return [[ref.at[i] for ref in refs] for i in range(RING)] if self.phase == 0 else [refs]
+            if self.kind == 1:
+                return grads.at[whose, half, at_z, :, self.lanes]
+            if self.kind == 2:
+                return grads.at[at_x, at_y, whose, :, self.fine[half]]
+            return grads.at[whose, at_y, at_z, :, self.fine[half]]
 
         def add(self, *refs):
-            for target, *others in self.pieces(refs):
-                total = target[...].astype(F32)
-                for other in others:
-                    total = total + other[...].astype(F32)
-                target[...] = total.astype(BF16)
+            if self.phase == 0:
+                for i in range(refs[1].shape[0]):
+                    add_up(*[ref.at[i] for ref in refs])
+            else:
+                add_up(*refs)
 
         def begin(self):
             for copy in self.copies[:4]:
@@ -256,40 +316,102 @@
             for copy in self.copies:
                 copy.wait_send()
 
-    rings = [[[Ring(stage, part, phase) for part in range(2)] for phase in range(2)] for stage in range(len(STAGES))]
-
-    def swap(stage, part):
-        begin, count = lanes_of(stage, part)
-        slot = len(STAGES) * 24 + stage * 2 + part
-        return pltpu.make_async_remote_copy(
-            src_ref=grads.at[at_x, 1 - at_y, at_z, :, pl.ds(begin * LEN, count * LEN)],
-            dst_ref=doubles[stage].at[part], send_sem=ring_out.at[slot], recv_sem=ring_in.at[slot],
-            device_id=across, device_id_type=pl.DeviceIdType.MESH,
-        )
-
-    def begin(stage, phase):
-        for ring in rings[stage][phase]:
-            ring.begin()
-
-    def relay(stage, phase):
-        for ring in rings[stage][phase]:
-            ring.relay()
-
-    def close(stage, phase):
-        for part, ring in enumerate(rings[stage][phase]):
-            ring.close()
-            if phase == 0:
-                rings[stage][1][part].begin()
+    def add_up(target, *others):
+        total = target[...].astype(F32)
+        for other in others:
+            total = total + other[...].astype(F32)
+        target[...] = total.astype(BF16)
+
+    class Piece:
+        def __init__(self, index):
+            kind, self.tile, self.count = PIECES[index]
+            self.lanes = pl.ds(self.tile * LEN, self.count * LEN)
+            self.early = kind >= 2
+            self.rings = [Ring(index, phase) for phase in range(2)]
+            self.landing = landings[3 * index + 2]
+            theirs = grads.at[:, 1 - at_y, :, :, self.lanes] if self.early else grads.at[at_x, 1 - at_y, at_z, :, self.lanes]
+            slot = index * 13 + 12
+            self.swap = remote(theirs, self.landing, ring_out.at[slot], ring_in.at[slot], across)
+
+        def open(self):
+            if self.early:
+                self.swap.start()
             else:
-                swap(stage, part).start()
+                self.rings[0].begin()
+
+        def join(self):
+            self.swap.wait_recv()
+
+            def one(i, carry):
+                for j in range(RING):
+                    add_up(grads.at[i, at_y, j, :, self.lanes], self.landing.at[i, j])
+                return carry
+
+            lax.fori_loop(0, RING, one, 0)
+            self.rings[0].begin()
+
+        def turn(self):
+            self.rings[0].close()
+            self.rings[1].begin()
+
+        def last(self):
+            self.rings[1].close()
+            if not self.early:
+                self.swap.start()
+
+        def settle(self):
+            total = grads[at_x, at_y, at_z, :, self.lanes].astype(F32)
+            if not self.early:
+                self.swap.wait_recv()
+                total = total + self.landing[...].astype(F32)
+            half = total.shape[0] // 2
+            for i in range(self.count):
+                here = slice(i * LEN, (i + 1) * LEN)
+                place_tile(self.tile + i, total[:half, here], total[half:, here])
+
+        def drain(self):
+            for ring in self.rings:
+                ring.drain()
+            self.swap.wait_send()
+
+    pieces, made = [], 0
+    for stage in PLAN:
+        pieces.append([Piece(made + i) for i in range(len(stage))])
+        made += len(stage)
+
+    def begin(stage):
+        for piece in pieces[stage]:
+            piece.open()
+
+    def relay(stage, phase, early):
+        for piece in pieces[stage]:
+            if piece.early == early:
+                piece.rings[phase].relay()
+
+    def turn(stage, early):
+        for piece in pieces[stage]:
+            if piece.early == early:
+                piece.turn()
+
+    def finish_rings(stage, early):
+        for piece in pieces[stage]:
+            if piece.early == early:
+                piece.last()
+
+    def join(stage):
+        for piece in pieces[stage]:
+            if piece.early:
+                piece.join()
+
+    def settle(stage):
+        for piece in pieces[stage]:
+            piece.settle()
 
     def place_tile(tile, top, bottom):
-        pair = pl.ds(tile % out_tiles * 2 * LEN, 2 * LEN)
-        if tile < out_tiles:
-            g_out[:, pair] = jnp.concatenate([top, bottom], axis=1)
-        elif tile < 2 * out_tiles:
-            within = (tile - out_tiles) * 2 * LEN
-            g_in[within // hidden, :, pl.ds(within % hidden, 2 * LEN)] = jnp.concatenate([top, bottom], axis=1)
+        if tile < 2 * out_tiles:
+            target = g_out if tile < out_tiles else g_in
+            within = tile % out_tiles * 2 * LEN
+            target[within // hidden, :, pl.ds(within % hidden, 2 * LEN)] = jnp.concatenate([top, bottom], axis=1)
         elif tile < 2 * out_tiles + 5:
             at_block = 2 * (tile - 2 * out_tiles)
             g_qkv[at_block // PAIRS, :, pl.ds(at_block % PAIRS * LEN, LEN)] = top
@@ -299,17 +421,6 @@
                 g_att[:, 2 * LEN :] = bottom
         else:
             g_att[:, : 2 * LEN] = jnp.concatenate([top, bottom], axis=1)
-
-    def settle(stage):
-        for part in range(2):
-            swap(stage, part).wait_recv()
-            begin_tile, count = lanes_of(stage, part)
-            lanes = pl.ds(begin_tile * LEN, count * LEN)
-            total = grads[at_x, at_y, at_z, :, lanes].astype(F32) + doubles[stage][part].astype(F32)
-            half = total.shape[0] // 2
-            for i in range(count):
-                here = slice(i * LEN, (i + 1) * LEN)
-                place_tile(begin_tile + i, total[:half, here], total[half:, here])
 
     def lot(slot, source, target, peer):
         return pltpu.make_async_remote_copy(
@@ -344,21 +455,38 @@
 
     def expert_gradients():
         product_tiles(0, rt, act2, out_tiles)
-        begin(0, 0)
+        begin(0)
         product_tiles(out_tiles, nt, back2, out_tiles)
-        begin(1, 0)
-
+        begin(1)
+
+    @pl.when(first)
+    def _():
+        for load in loads_first:
+            load.wait()
+
+    @pl.when(last)
+    def _():
+        for load in loads_last[:2]:
+            load.wait_recv()
+
+    split = router[0:1, :] - router[1:2, :]
+
+    def column(values):
+        return jnp.broadcast_to(values, (LEN, LEN)).T[:, :1]
+
+    def sign_rows(c, carry):
+        for s in range(SEQS):
+            signs[c, pl.ds(s * LEN, LEN), :] = column((1 - 2 * routes[c * SEQS + s]).astype(F32))
+        return carry
+
+    lax.fori_loop(0, chunks, sign_rows, 0)
     for load in loads:
         load.wait()
 
-    @pl.when(first)
-    def _():
-        load_x.wait()
-
     def forward(c, carry):
         @pl.when(last)
         def _():
-            forward_copy(c).wait_recv()
+            land(forward_copy(c))
 
         spot = pl.multiple_of(c * rows, rows)
         here = pl.ds(spot, rows)
@@ -389,13 +517,12 @@
         scale = lax.rsqrt(jnp.mean(a * a, axis=1, keepdims=True) + epsilon)
         normed2 = (a * scale * gain_f[...]).astype(BF16)
         nt[:, here] = normed2.T
-        route = routes[c]
-        sign = (1 - 2 * route).astype(F32)
-        logit = over_lanes(normed2.astype(F32) * rdiff[...])
+        sign = signs[c]
+        logit = over_lanes(normed2.astype(F32) * split)
         chosen = 1.0 / (1.0 + jnp.exp(-sign * logit))
         chosens[c] = chosen
-        to_zero = (route == 0).astype(BF16)
-        to_one = (route == 1).astype(BF16)
+        to_zero = (sign > 0).astype(BF16)
+        to_one = (sign < 0).astype(BF16)
         doubled = jnp.concatenate([normed2 * to_zero, normed2 * to_one], axis=1)
 
         def inner_tile(n, carry):
@@ -420,7 +547,9 @@
 
         @pl.when(first)
         def _():
-            forward_copy(c).start()
+            cross(forward_copy(c))
+
+        give_start(give(sec, sec_hbm, c, 0))
 
         return carry
 
@@ -428,20 +557,19 @@
 
     @pl.when(last)
     def _():
-        load_dy.wait()
+        loads_last[2].wait_recv()
 
     def backward(c, carry):
         @pl.when(first)
         def _():
-            backward_copy(c).wait_recv()
+            land(backward_copy(c))
 
         spot = pl.multiple_of(c * rows, rows)
         here = pl.ds(spot, rows)
         dy = dys[c].astype(F32)
-        route = routes[c]
-        sign = (1 - 2 * route).astype(F32)
-        to_zero = (route == 0).astype(BF16)
-        to_one = (route == 1).astype(BF16)
+        sign = signs[c]
+        to_zero = (sign > 0).astype(BF16)
+        to_one = (sign < 0).astype(BF16)
         chosen = chosens[c]
         d_logit = sign * over_lanes(dy * result[here, :].astype(F32)) * chosen * (1.0 - chosen)
         d_result = (chosen * dy).astype(BF16)
@@ -469,7 +597,7 @@
         d_normed2 = dot(back2[here, :hidden], win[:width, :], NT) + dot(
             back2[here, hidden:], win[width:, :], NT
         )
-        d_normed2 = exchanged(4 * c + 2, d_normed2) + d_logit * rdiff[...]
+        d_normed2 = exchanged(4 * c + 2, d_normed2) + d_logit * split
         a = after[here, :]
         scale = lax.rsqrt(jnp.mean(a * a, axis=1, keepdims=True) + epsilon)
         plain = a * scale
@@ -516,7 +644,9 @@
 
         @pl.when(last)
         def _():
-            backward_copy(c).start()
+            cross(backward_copy(c))
+
+        give_start(give(dgrad, dgrad_hbm, c, 1))
 
         return carry
 
@@ -531,60 +661,99 @@
         for pair in range(PAIRS):
             for side in range(2):
                 picked = jnp.where(hit, dsum[pair, :, pl.ds(side * LEN, LEN)], 0.0)
-                tables[pl.ds((2 * pair + side) * buckets + b, 1), :] = over_rows(picked)
+                tables[pl.ds((2 * pair + side) * LEN + b, 1), :] = over_rows(picked)
         return carry
 
     lax.fori_loop(0, buckets, table_rows, 0)
-    own[0, 3:4, : 2 * LEN] = over_rows(tables[...].T)
+    own[0, 3:4, :] = over_rows(tables[...].T)
     lots_open(0)
-    relay(0, 0)
+    relay(0, 0, False)
     product_tiles(2 * out_tiles, xt, dproj, 4)
     keep(2 * out_tiles + 4, dot(xt[...], dproj[:, 8 * LEN :]), dot(at[...], mixed[:, 2 * LEN :]))
     made = dot(at[...], mixed[:, : 2 * LEN])
     keep(2 * out_tiles + 5, made[:, :LEN], made[:, LEN:])
-    begin(2, 0)
+    begin(2)
+    join(0)
     lots_pass(0)
-    relay(1, 0)
+    relay(1, 0, False)
     lots_sum(0)
     lots_open(1)
-    close(0, 0)
+    turn(0, False)
+    join(1)
+    relay(0, 0, True)
     lots_pass(1)
-    relay(2, 0)
+    relay(2, 0, False)
     lots_sum(1)
     lot_copies[6].start()
-    relay(0, 1)
-    close(1, 0)
-    close(0, 1)
-    relay(1, 1)
-    close(2, 0)
+    relay(0, 1, False)
+    turn(1, False)
+    turn(0, True)
+    relay(1, 0, True)
+    finish_rings(0, False)
+    relay(1, 1, False)
+    turn(2, False)
+    relay(0, 1, True)
+    turn(1, True)
+    finish_rings(1, False)
+    relay(2, 1, False)
+    finish_rings(0, True)
     settle(0)
-    close(1, 1)
-    relay(2, 1)
+    relay(1, 1, True)
+    finish_rings(2, False)
+    finish_rings(1, True)
     settle(1)
     lot_copies[6].wait_recv()
-    small[...] = own[2] + lots[8]
-    close(2, 1)
+    small = own[2] + lots[8]
+    g_gain_a[...] = small[0:1, :]
+    g_gain_f[...] = small[1:2, :]
+    g_router[0:1, :] = small[2:3, :]
+    g_router[1:2, :] = -small[2:3, :]
+    for head in range(2 * PAIRS):
+        g_table[head] = small[3:4, head * LEN : head * LEN + buckets]
     settle(2)
     for copy in lot_copies:
         copy.wait_send()
-    for stage in range(len(STAGES)):
-        for part in range(2):
-            rings[stage][0][part].drain()
-            rings[stage][1][part].drain()
-            swap(stage, part).wait_send()
+    for stage in pieces:
+        for piece in stage:
+            piece.drain()
+
+    @pl.when(last)
+    def _():
+        for load in loads_last:
+            load.wait_send()
 
     def finish(c, carry):
+        give_wait(give(sec, sec_hbm, c, 0))
+        give_wait(give(dgrad, dgrad_hbm, c, 1))
+
         @pl.when(first)
         def _():
-            forward_copy(c).wait_send()
+            for copy in forward_copy(c)[0] + backward_copy(c)[1]:
+                copy.wait_send()
 
         @pl.when(last)
         def _():
-            backward_copy(c).wait_send()
+            for copy in backward_copy(c)[0] + forward_copy(c)[1]:
+                copy.wait_send()
 
         return carry
 
     lax.fori_loop(0, chunks, finish, 0)
+
+
+def copy_out(*refs):
+    count = len(refs) // 3
+    sources, targets, held = refs[:count], refs[count : 2 * count], refs[2 * count : 3 * count]
+    sem_in, sem_out = refs[3 * count :]
+    arrive = [pltpu.make_async_copy(*ends, sem_in.at[i]) for i, ends in enumerate(zip(sources, held))]
+    leave = [pltpu.make_async_copy(*ends, sem_out.at[i]) for i, ends in enumerate(zip(held, targets))]
+    for copy in arrive:
+        copy.start()
+    for first, second in zip(arrive, leave):
+        first.wait()
+        second.start()
+    for copy in leave:
+        copy.wait()
 
 
 def local_pass(inputs, cotangent, segments, routes, gain_attn, w_qkv, rel_table, w_att_out, gain_ffn, router, w_in, w_out):
@@ -594,7 +763,8 @@
     tokens = micros * length
     experts, _, hidden = w_in.shape
     heads = w_att_out.shape[0]
-    buckets = rel_table.shape[0]
+    buckets = rel_table.shape[1]
+    count = len(PIECES)
     columns = (3 * heads + heads + 2 * experts * hidden) // 2
     vmem = pl.BlockSpec(memory_space=pltpu.VMEM)
     smem = pl.BlockSpec(memory_space=pltpu.SMEM)
@@ -602,8 +772,19 @@
     slots = 4 * chunks
     shard = width // (2 * RING * RING)
     double = 2 * shard
-    pieces = [(end - begin) // 2 * LEN for begin, end in STAGES]
+    landings = []
+    for kind, _, tiles in PIECES:
+        wide = tiles * LEN
+        if kind < 2:
+            landings += [(6, RING, double, wide), (6, double, wide), (double, wide)]
+        else:
+            landings += [(6, 2, double, wide), (6, double, wide // 2), (RING, RING, double, wide)]
     scratch = [
+        pltpu.VMEM((micros, length), jnp.int32),
+        pltpu.VMEM((micros, 1, length), jnp.int32),
+        pltpu.VMEM((chunks, rows, 1), F32),
+        pltpu.VMEM((chunks, rows, width), BF16),
+        pltpu.VMEM((chunks, rows, width), BF16),
         pltpu.VMEM(w_qkv.shape, BF16),
         pltpu.VMEM(w_att_out.shape, BF16),
         pltpu.VMEM((experts * width, hidden), BF16),
@@ -628,36 +809,41 @@
         pltpu.VMEM((slots, rows, width), BF16),
         pltpu.VMEM((PAIRS, LEN, 2 * LEN), F32),
         pltpu.VMEM((PAIRS, LEN, 2 * LEN), F32),
-        pltpu.VMEM((2 * LEN, LEN), F32),
+        pltpu.VMEM((2 * PAIRS * LEN, LEN), F32),
         pltpu.VMEM((RING, 2, RING, double, columns), BF16),
-        *[pltpu.VMEM((2, 6, RING, double, piece), BF16) for piece in pieces],
-        *[pltpu.VMEM((2, 6, double, piece), BF16) for piece in pieces],
-        *[pltpu.VMEM((2, double, piece), BF16) for piece in pieces],
         pltpu.VMEM((3, 8, width), F32),
         pltpu.VMEM((9, 8, width), F32),
-        pltpu.SemaphoreType.DMA((5,)),
+        pltpu.SemaphoreType.DMA((7 + 2 * chunks,)),
         pltpu.SemaphoreType.DMA((slots,)),
         pltpu.SemaphoreType.DMA((slots,)),
-        pltpu.SemaphoreType.DMA((2 * chunks,)),
-        pltpu.SemaphoreType.DMA((2 * chunks,)),
-        pltpu.SemaphoreType.DMA((26 * len(STAGES),)),
-        pltpu.SemaphoreType.DMA((26 * len(STAGES),)),
+        pltpu.SemaphoreType.DMA((2 * chunks * CUTS,)),
+        pltpu.SemaphoreType.DMA((2 * chunks * CUTS,)),
+        pltpu.SemaphoreType.DMA((2 * chunks * CUTS,)),
+        pltpu.SemaphoreType.DMA((2 * chunks * CUTS,)),
+        pltpu.SemaphoreType.DMA((3 + 2 * chunks,)),
+        pltpu.SemaphoreType.DMA((3 + 2 * chunks,)),
+        pltpu.SemaphoreType.DMA((13 * count,)),
+        pltpu.SemaphoreType.DMA((13 * count,)),
         pltpu.SemaphoreType.DMA((7,)),
         pltpu.SemaphoreType.DMA((7,)),
+        *[pltpu.VMEM(shape, BF16) for shape in landings],
     ]
-    return pl.pallas_call(
+    results = pl.pallas_call(
         kernel,
         out_shape=[
             jax.ShapeDtypeStruct((chunks, rows, width), BF16),
             jax.ShapeDtypeStruct((chunks, rows, width), BF16),
-            jax.ShapeDtypeStruct((shard, experts * hidden), F32),
+            jax.ShapeDtypeStruct((experts, shard, hidden), F32),
             jax.ShapeDtypeStruct((experts, shard, hidden), F32),
             jax.ShapeDtypeStruct((3, shard, heads), F32),
             jax.ShapeDtypeStruct((shard, heads), F32),
-            jax.ShapeDtypeStruct((8, width), F32),
+            jax.ShapeDtypeStruct((1, width), F32),
+            jax.ShapeDtypeStruct((1, width), F32),
+            jax.ShapeDtypeStruct((2, width), F32),
+            jax.ShapeDtypeStruct((2 * PAIRS, 1, buckets), F32),
         ],
-        in_specs=[anywhere, anywhere, vmem, vmem, vmem, smem, vmem, vmem] + [anywhere] * 4,
-        out_specs=[vmem] * 7,
+        in_specs=[anywhere] * 4 + [vmem, smem, vmem, vmem] + [anywhere] * 4,
+        out_specs=[anywhere] * 2 + [vmem] * 8,
         scratch_shapes=scratch,
         compiler_params=pltpu.CompilerParams(
             collective_id=0, has_side_effects=True, vmem_limit_bytes=62 * 2**20
@@ -667,42 +853,46 @@
         inputs.reshape(chunks, rows, width),
         cotangent.reshape(chunks, rows, width),
         segments,
-        routes.reshape(chunks, rows, 1),
+        jnp.swapaxes(routes, 1, 2),
         gain_attn,
-        rel_table,
+        jnp.transpose(rel_table, (2, 0, 1)),
         gain_ffn,
-        (router[:, 0] - router[:, 1])[None, :],
+        router.T,
         w_qkv,
         w_att_out,
         w_in.reshape(experts * width, hidden),
         w_out.reshape(experts * hidden, width),
     )
+    return pl.pallas_call(
+        copy_out,
+        out_shape=[jax.ShapeDtypeStruct(made.shape, made.dtype) for made in results],
+        in_specs=[anywhere] * len(results),
+        out_specs=[anywhere] * len(results),
+        scratch_shapes=[pltpu.VMEM(made.shape, made.dtype) for made in results]
+        + [pltpu.SemaphoreType.DMA((len(results),))] * 2,
+    )(*results)
 
 
 def per_device(
     inputs, cotangent, segments, routes, gain_attn, w_qkv, rel_table, w_att_out, gain_ffn, router, w_in, w_out
 ):
     experts, width, hidden = w_in.shape[1:]
-    sec, dgrad, g_out, g_in, g_qkv, g_att, small = local_pass(
-        inputs, cotangent, segments, routes[0], gain_attn, w_qkv[0], rel_table[0], w_att_out[0],
+    sec, dgrad, g_out, g_in, g_qkv, g_att, gain_a, gain_f, g_router, table = local_pass(
+        inputs, cotangent, segments, routes[0], gain_attn, w_qkv[0], rel_table, w_att_out[0],
         gain_ffn, router[0], w_in[0], w_out[0],
     )
-    buckets, heads = rel_table.shape[1:]
-    g_out = g_out.reshape(-1, experts, hidden).transpose(1, 2, 0)
-    gain_a, gain_f, routed = small[0], small[1], small[2]
-    table = small[3, : buckets * heads].reshape(heads, buckets).T
     micros, length = inputs.shape[:2]
     return (
         sec.reshape(1, micros, length, width),
         dgrad.reshape(1, micros, length, width),
-        gain_a[None],
+        gain_a,
         g_qkv[None],
-        table[None],
+        jnp.transpose(table, (1, 2, 0)),
         g_att.T[None],
-        gain_f[None],
-        jnp.stack([routed, -routed], axis=1)[None],
+        gain_f,
+        g_router.T[None],
         g_in[None],
-        g_out[None],
+        jnp.swapaxes(g_out, 1, 2)[None],
     )
 
 

time: 183 us -> 152 us (0.83)
  local copies, waits for them, and re-layouts: 16.1 us -> 0 us
  Pallas kernels: 161 us -> 151 us
  other arithmetic: 4.04 us -> 0 us
    pallas_call x1, Pallas kernels: 161 us -> 148 us  [local_pass(): pl.pallas_call(kernel, out_shape=[jax.ShapeDtypeStruct((chunks, rows, wid...]
    unnamed x7 -> x0, local copies, waits for them, and re-layouts: 10.6 us -> none
    pallas_call x0 -> x1, Pallas kernels: none -> 2.69 us  [local_pass(): pl.pallas_call(copy_out, out_shape=[jax.ShapeDtypeStruct(made.shape, made...]
    another operation x3 -> x0, local copies, waits for them, and re-layouts: 2.43 us -> none  [the longest x1 1.44 us: per_device(): jnp.stack([routed, -routed], axis=1)[None]]
where the time goes in v3:
time: 152 us
  Pallas kernels  151 us (99%)
    pallas_call x1, Pallas kernels, local_pass(): pl.pallas_call(kernel, out_shape=[jax.ShapeDtypeStruct((chunks, rows, wid...  148 us

profile of v3, /device:TPU:0, one launch (start us, length us, event | category | flops | bytes accessed | tf_op | source)
XLA Modules:
  0.0 151.9 jit_solution(2377480652808887479)
XLA Ops:
  0.6 148.4 %shard_map.195 = (bf16[2,256,768]{2,1,0:T(8,128)(2,1)}, bf16[2,256,768]{2,1,0:T(8,128)(2,1)}, f32[2,24,1536]{2,1,0:T(8,128)}, f32[2,24,1536]{2,1,0:T(8,128)}, f3...) custom-call(bf16[2,256,768]{2,1,0:T(8,128)(2,1)} %bitcast.28, ...), custom_call_target="tpu_custom_call" | custom-call | flops 17999998976 | bytes 30000000 | tf_op jit(solution)/shard_map/pallas_call | solution.py:831
  149.0 2.7 %shard_map.196 = (bf16[2,256,768]{2,1,0:T(8,128)(2,1)}, bf16[2,256,768]{2,1,0:T(8,128)(2,1)}, f32[2,24,1536]{2,1,0:T(8,128)}, f32[2,24,1536]{2,1,0:T(8,128)}, f3...) custom-call(bf16[2,256,768]{2,1,0:T(8,128)(2,1)} %get-tuple-element., ...), custom_call_target="tpu_custom_call" | custom-call | tf_op jit(solution)/shard_map/pallas_call | solution.py:866

commit v4 on v3

--- a/solution.py
+++ b/solution.py
@@ -77,7 +77,6 @@
     last = pipe == 1
     chunks, rows, width = hs.shape
     hidden = slope.shape[-1]
-    step = 512
     buckets = table.shape[-1]
 
     loads = [
@@ -134,8 +133,12 @@
         for load in loads_last:
             load.start()
 
-    def to_other_core(slot):
-        return remote(send, recv.at[slot], out_sem.at[slot], in_sem.at[slot], other_core)
+    def exchanged(slot, part):
+        send[...] = part.astype(BF16)
+        copy = remote(send, recv.at[slot % 2], out_sem.at[slot], in_sem.at[slot], other_core)
+        copy.start()
+        copy.wait()
+        return send[...].astype(F32) + recv[slot % 2].astype(F32)
 
     def crossing(source, target, c, back):
         length = rows // (2 * CUTS)
@@ -192,13 +195,6 @@
         def _():
             given[1].wait()
 
-    def exchanged(slot, part):
-        send[...] = part.astype(BF16)
-        copy = to_other_core(slot)
-        copy.start()
-        copy.wait()
-        return send[...].astype(F32) + recv[slot].astype(F32)
-
     bucket = bucket_map(buckets)
     lane = lax.broadcasted_iota(jnp.int32, (LEN, LEN), 1)
     upper = lane >= HEAD
@@ -240,12 +236,13 @@
 
     def product_tiles(tile, lefts, rights, count):
         def one(n, carry):
-            lanes = pl.ds(pl.multiple_of(n * 2 * LEN, 2 * LEN), 2 * LEN)
+            lanes = pl.ds(pl.multiple_of(n * 4 * LEN, 4 * LEN), 4 * LEN)
             made = dot(lefts[...], rights[:, lanes])
-            keep(tile + n, made[:, :LEN], made[:, LEN:])
+            keep(tile + 2 * n, made[:, :LEN], made[:, LEN : 2 * LEN])
+            keep(tile + 2 * n + 1, made[:, 2 * LEN : 3 * LEN], made[:, 3 * LEN :])
             return carry
 
-        lax.fori_loop(0, count, one, 0)
+        lax.fori_loop(0, count // 2, one, 0)
 
     out_tiles = 2 * hidden // (2 * LEN)
     class Ring:
@@ -453,11 +450,14 @@
         base = 4 * phase
         own[phase + 1] = (own[phase] + lots[base + 2]) + (lots[base] + lots[base + 1])
 
-    def expert_gradients():
+    def out_gradients():
         product_tiles(0, rt, act2, out_tiles)
         begin(0)
+
+    def in_gradients():
         product_tiles(out_tiles, nt, back2, out_tiles)
         begin(1)
+        relay(0, 0, False)
 
     @pl.when(first)
     def _():
@@ -480,7 +480,7 @@
         return carry
 
     lax.fori_loop(0, chunks, sign_rows, 0)
-    for load in loads:
+    for load in loads[:2]:
         load.wait()
 
     def forward(c, carry):
@@ -525,22 +525,20 @@
         to_one = (sign < 0).astype(BF16)
         doubled = jnp.concatenate([normed2 * to_zero, normed2 * to_one], axis=1)
 
-        def inner_tile(n, carry):
-            lanes = pl.ds(pl.multiple_of(n * step, step), step)
-            inner = dot(doubled, win[:, lanes])
-            squared = inner * inner
-            root = np.sqrt(2 / np.pi).astype(np.float32)
-            bend = jnp.tanh(root * inner * (1.0 + 0.044715 * squared))
-            steep = 0.5 * (1.0 + bend) + 0.5 * inner * (1.0 - bend * bend) * root * (
-                1.0 + 3 * 0.044715 * squared
-            )
-            slope[here, lanes] = steep.astype(BF16)
-            active = (0.5 * inner * (1.0 + bend)).astype(BF16)
-            act2[here, lanes] = active * to_zero
-            act2[here, pl.ds(pl.multiple_of(hidden + n * step, step), step)] = active * to_one
-            return carry
-
-        lax.fori_loop(0, hidden // step, inner_tile, 0)
+        @pl.when(c == 0)
+        def _():
+            for load in loads[2:]:
+                load.wait()
+
+        inner = dot(doubled, win[...])
+        squared = inner * inner
+        root = np.sqrt(2 / np.pi).astype(np.float32)
+        bend = jnp.tanh(root * inner * (1.0 + 0.044715 * squared))
+        steep = 0.5 * (1.0 + bend) + 0.5 * inner * (1.0 - bend * bend) * root * (1.0 + 3 * 0.044715 * squared)
+        slope[here, :] = steep.astype(BF16)
+        active = (0.5 * inner * (1.0 + bend)).astype(BF16)
+        act2[here, :hidden] = active * to_zero
+        act2[here, hidden:] = active * to_one
         total = exchanged(4 * c + 1, dot(act2[here, :], wout[...]))
         result[here, :] = total.astype(BF16)
         sec[c] = (after[here, :] + chosen * total).astype(BF16)
@@ -577,27 +575,24 @@
         zero_part = d_result * to_zero
         one_part = d_result * to_one
 
-        def active_tile(n, carry):
-            low = pl.multiple_of(n * step, step)
-            high = pl.multiple_of(hidden + n * step, step)
-            d_active = dot(zero_part, wout[pl.ds(low, step), :], NT) + dot(
-                one_part, wout[pl.ds(high, step), :], NT
-            )
-            d_inner = (d_active * slope[here, pl.ds(low, step)].astype(F32)).astype(BF16)
-            back2[here, pl.ds(low, step)] = d_inner * to_zero
-            back2[here, pl.ds(high, step)] = d_inner * to_one
-            return carry
-
-        lax.fori_loop(0, hidden // step, active_tile, 0)
-
         @pl.when(first & (c == chunks - 1))
         def _():
-            expert_gradients()
+            out_gradients()
+
+        d_active = dot(zero_part, wout[:hidden, :], NT) + dot(one_part, wout[hidden:, :], NT)
+        d_inner = (d_active * slope[here, :].astype(F32)).astype(BF16)
+        back2[here, :hidden] = d_inner * to_zero
+        back2[here, hidden:] = d_inner * to_one
+
+        @pl.when(first & (c == chunks - 1))
+        def _():
+            in_gradients()
 
         d_normed2 = dot(back2[here, :hidden], win[:width, :], NT) + dot(
             back2[here, hidden:], win[width:, :], NT
         )
-        d_normed2 = exchanged(4 * c + 2, d_normed2) + d_logit * split
+        d_normed2 = exchanged(4 * c + 2, d_normed2)
+        d_normed2 = d_normed2 + d_logit * split
         a = after[here, :]
         scale = lax.rsqrt(jnp.mean(a * a, axis=1, keepdims=True) + epsilon)
         plain = a * scale
@@ -654,7 +649,8 @@
 
     @pl.when(last)
     def _():
-        expert_gradients()
+        out_gradients()
+        in_gradients()
 
     def table_rows(b, carry):
         hit = bucket == b
@@ -667,39 +663,38 @@
     lax.fori_loop(0, buckets, table_rows, 0)
     own[0, 3:4, :] = over_rows(tables[...].T)
     lots_open(0)
-    relay(0, 0, False)
     product_tiles(2 * out_tiles, xt, dproj, 4)
     keep(2 * out_tiles + 4, dot(xt[...], dproj[:, 8 * LEN :]), dot(at[...], mixed[:, 2 * LEN :]))
     made = dot(at[...], mixed[:, : 2 * LEN])
     keep(2 * out_tiles + 5, made[:, :LEN], made[:, LEN:])
     begin(2)
-    join(0)
     lots_pass(0)
     relay(1, 0, False)
     lots_sum(0)
     lots_open(1)
+    join(0)
     turn(0, False)
-    join(1)
-    relay(0, 0, True)
     lots_pass(1)
     relay(2, 0, False)
     lots_sum(1)
     lot_copies[6].start()
+    relay(0, 0, True)
+    turn(1, False)
+    join(1)
     relay(0, 1, False)
-    turn(1, False)
     turn(0, True)
+    turn(2, False)
+    relay(1, 1, False)
     relay(1, 0, True)
     finish_rings(0, False)
-    relay(1, 1, False)
-    turn(2, False)
     relay(0, 1, True)
+    relay(2, 1, False)
     turn(1, True)
     finish_rings(1, False)
-    relay(2, 1, False)
     finish_rings(0, True)
     settle(0)
+    finish_rings(2, False)
     relay(1, 1, True)
-    finish_rings(2, False)
     finish_rings(1, True)
     settle(1)
     lot_copies[6].wait_recv()
@@ -806,7 +801,7 @@
         pltpu.VMEM((chunks, rows, 1), F32),
         pltpu.VMEM((tokens, 3 * heads), BF16),
         pltpu.VMEM((rows, width), BF16),
-        pltpu.VMEM((slots, rows, width), BF16),
+        pltpu.VMEM((2, rows, width), BF16),
         pltpu.VMEM((PAIRS, LEN, 2 * LEN), F32),
         pltpu.VMEM((PAIRS, LEN, 2 * LEN), F32),
         pltpu.VMEM((2 * PAIRS * LEN, LEN), F32),

time: 152 us -> 149 us (0.980)
  Pallas kernels: 151 us -> 148 us
    pallas_call x1, Pallas kernels: 148 us -> 145 us  [local_pass(): pl.pallas_call(kernel, out_shape=[jax.ShapeDtypeStruct((chunks, rows, wid...]
where the time goes in v4:
time: 149 us; the launch traced here: 148 us
  Pallas kernels  148 us (99%)
    pallas_call x1, Pallas kernels, local_pass(): pl.pallas_call(kernel, out_shape=[jax.ShapeDtypeStruct((chunks, rows, wid...  145 us

profile of v4, /device:TPU:0, one launch (start us, length us, event | category | flops | bytes accessed | tf_op | source)
XLA Modules:
  0.0 148.4 jit_solution(11504987405786468036)
XLA Ops:
  0.6 144.9 %shard_map.195 = (bf16[2,256,768]{2,1,0:T(8,128)(2,1)}, bf16[2,256,768]{2,1,0:T(8,128)(2,1)}, f32[2,24,1536]{2,1,0:T(8,128)}, f32[2,24,1536]{2,1,0:T(8,128)}, f3...) custom-call(bf16[2,256,768]{2,1,0:T(8,128)(2,1)} %bitcast.28, ...), custom_call_target="tpu_custom_call" | custom-call | flops 17999998976 | bytes 30000000 | tf_op jit(solution)/shard_map/pallas_call | solution.py:826
  145.5 2.7 %shard_map.196 = (bf16[2,256,768]{2,1,0:T(8,128)(2,1)}, bf16[2,256,768]{2,1,0:T(8,128)(2,1)}, f32[2,24,1536]{2,1,0:T(8,128)}, f32[2,24,1536]{2,1,0:T(8,128)}, f3...) custom-call(bf16[2,256,768]{2,1,0:T(8,128)(2,1)} %get-tuple-element., ...), custom_call_target="tpu_custom_call" | custom-call | tf_op jit(solution)/shard_map/pallas_call | solution.py:861

commit v5 on v4

--- a/solution.py
+++ b/solution.py
@@ -95,7 +95,7 @@
         for load in loads_first:
             load.start()
 
-    for load in loads:
+    for load in loads[:2]:
         load.start()
 
     barrier = pltpu.get_barrier_semaphore()
@@ -120,7 +120,6 @@
 
     for peer in peers:
         pl.semaphore_signal(barrier, inc=1, device_id=peer, device_id_type=pl.DeviceIdType.MESH)
-    pl.semaphore_wait(barrier, 1 + len(peers))
 
     other_core = {"tensor": 1 - tensor}
     loads_last = [
@@ -128,17 +127,13 @@
         for i, (source, target) in enumerate(((segs_hbm, segs), (routes_hbm, routes), (dy_hbm, dys)))
     ]
 
-    @pl.when(last)
-    def _():
-        for load in loads_last:
-            load.start()
-
-    def exchanged(slot, part):
+    def exchanged(slot, part, meanwhile=lambda: None):
         send[...] = part.astype(BF16)
         copy = remote(send, recv.at[slot % 2], out_sem.at[slot], in_sem.at[slot], other_core)
         copy.start()
+        beside = meanwhile()
         copy.wait()
-        return send[...].astype(F32) + recv[slot % 2].astype(F32)
+        return send[...].astype(F32) + recv[slot % 2].astype(F32), beside
 
     def crossing(source, target, c, back):
         length = rows // (2 * CUTS)
@@ -212,6 +207,12 @@
         return carry
 
     lax.fori_loop(0, buckets, add_bias, 0)
+    pl.semaphore_wait(barrier, 1 + len(peers))
+
+    @pl.when(last)
+    def _():
+        for load in loads_last:
+            load.start()
 
     def stacked(values):
         zero = jnp.zeros_like(values)
@@ -234,9 +235,9 @@
         both = jnp.concatenate([left, right], axis=3).astype(BF16)
         grads[:, :, :, :, pl.ds(pl.multiple_of(tile * LEN, LEN), LEN)] = both
 
-    def product_tiles(tile, lefts, rights, count):
+    def product_tiles(tile, lefts, rights, count, skip=0):
         def one(n, carry):
-            lanes = pl.ds(pl.multiple_of(n * 4 * LEN, 4 * LEN), 4 * LEN)
+            lanes = pl.ds(pl.multiple_of(skip * 2 * LEN + n * 4 * LEN, 4 * LEN), 4 * LEN)
             made = dot(lefts[...], rights[:, lanes])
             keep(tile + 2 * n, made[:, :LEN], made[:, LEN : 2 * LEN])
             keep(tile + 2 * n + 1, made[:, 2 * LEN : 3 * LEN], made[:, 3 * LEN :])
@@ -451,8 +452,14 @@
         own[phase + 1] = (own[phase] + lots[base + 2]) + (lots[base] + lots[base + 1])
 
     def out_gradients():
-        product_tiles(0, rt, act2, out_tiles)
-        begin(0)
+        done = 0
+        for piece in pieces[0]:
+            if piece.tile + piece.count > done:
+                until = piece.tile + piece.count
+                until += until % 4
+                product_tiles(done, rt, act2, until - done, done)
+                done = until
+            piece.open()
 
     def in_gradients():
         product_tiles(out_tiles, nt, back2, out_tiles)
@@ -482,6 +489,8 @@
     lax.fori_loop(0, chunks, sign_rows, 0)
     for load in loads[:2]:
         load.wait()
+    for load in loads[2:]:
+        load.start()
 
     def forward(c, carry):
         @pl.when(last)
@@ -512,11 +521,10 @@
                 prob = raised / per_head(raised, jnp.sum)
                 probs[c * SEQS + s, pair] = prob
                 mixed[seq, lanes] = dot(prob.astype(BF16), values).astype(BF16)
-        a = h + exchanged(4 * c, dot(mixed[here, :], watt[...]))
+        a = h + exchanged(4 * c, dot(mixed[here, :], watt[...]))[0]
         after[here, :] = a
         scale = lax.rsqrt(jnp.mean(a * a, axis=1, keepdims=True) + epsilon)
         normed2 = (a * scale * gain_f[...]).astype(BF16)
-        nt[:, here] = normed2.T
         sign = signs[c]
         logit = over_lanes(normed2.astype(F32) * split)
         chosen = 1.0 / (1.0 + jnp.exp(-sign * logit))
@@ -530,16 +538,29 @@
             for load in loads[2:]:
                 load.wait()
 
-        inner = dot(doubled, win[...])
-        squared = inner * inner
         root = np.sqrt(2 / np.pi).astype(np.float32)
-        bend = jnp.tanh(root * inner * (1.0 + 0.044715 * squared))
-        steep = 0.5 * (1.0 + bend) + 0.5 * inner * (1.0 - bend * bend) * root * (1.0 + 3 * 0.044715 * squared)
-        slope[here, :] = steep.astype(BF16)
-        active = (0.5 * inner * (1.0 + bend)).astype(BF16)
-        act2[here, :hidden] = active * to_zero
-        act2[here, hidden:] = active * to_one
-        total = exchanged(4 * c + 1, dot(act2[here, :], wout[...]))
+
+        def half_of(value, squared):
+            return 0.5 * (1.0 + jnp.tanh(root * value * (1.0 + 0.044715 * squared)))
+
+        sides = [(pl.ds(i * (hidden // 2), hidden // 2), pl.ds(hidden + i * (hidden // 2), hidden // 2)) for i in range(2)]
+        for low, high in sides:
+            value = dot(doubled, win[:, low])
+            slope[here, low] = value.astype(BF16)
+            active = (value * half_of(value, value * value)).astype(BF16)
+            act2[here, low] = active * to_zero
+            act2[here, high] = active * to_one
+
+        def slopes():
+            nt[:, here] = normed2.T
+            for low, _ in sides:
+                value = slope[here, low].astype(F32)
+                squared = value * value
+                half = half_of(value, squared)
+                steep = half + 2.0 * value * half * (1.0 - half) * (root * (1.0 + 3 * 0.044715 * squared))
+                slope[here, low] = steep.astype(BF16)
+
+        total, _ = exchanged(4 * c + 1, dot(act2[here, :], wout[...]), slopes)
         result[here, :] = total.astype(BF16)
         sec[c] = (after[here, :] + chosen * total).astype(BF16)
 
@@ -591,14 +612,18 @@
         d_normed2 = dot(back2[here, :hidden], win[:width, :], NT) + dot(
             back2[here, hidden:], win[width:, :], NT
         )
-        d_normed2 = exchanged(4 * c + 2, d_normed2)
+
+        def unit_after():
+            a = after[here, :]
+            scale = lax.rsqrt(jnp.mean(a * a, axis=1, keepdims=True) + epsilon)
+            plain = a * scale
+            normed2 = (plain * gain_f[...]).astype(BF16).astype(F32)
+            own[0, 2:3, :] += over_rows(normed2 * d_logit)
+            return scale, plain
+
+        d_normed2, (scale, plain) = exchanged(4 * c + 2, d_normed2, unit_after)
         d_normed2 = d_normed2 + d_logit * split
-        a = after[here, :]
-        scale = lax.rsqrt(jnp.mean(a * a, axis=1, keepdims=True) + epsilon)
-        plain = a * scale
-        normed2 = (plain * gain_f[...]).astype(BF16).astype(F32)
         own[0, 1:2, :] += over_rows(d_normed2 * plain)
-        own[0, 2:3, :] += over_rows(normed2 * d_logit)
         pulled = d_normed2 * gain_f[...]
         d_after = dy + scale * (pulled - plain * jnp.mean(pulled * plain, axis=1, keepdims=True))
         after[here, :] = d_after
@@ -626,10 +651,13 @@
         d_normed = dot(dproj[here, :part], wqkv[0], NT)
         d_normed = d_normed + dot(dproj[here, part : 2 * part], wqkv[1], NT)
         d_normed = d_normed + dot(dproj[here, 2 * part :], wqkv[2], NT)
-        d_normed = exchanged(4 * c + 3, d_normed)
-        h = hs[c].astype(F32)
-        scale = lax.rsqrt(jnp.mean(h * h, axis=1, keepdims=True) + epsilon)
-        plain = h * scale
+
+        def unit_hidden():
+            h = hs[c].astype(F32)
+            scale = lax.rsqrt(jnp.mean(h * h, axis=1, keepdims=True) + epsilon)
+            return scale, h * scale
+
+        d_normed, (scale, plain) = exchanged(4 * c + 3, d_normed, unit_hidden)
         own[0, 0:1, :] += over_rows(d_normed * plain)
         pulled = d_normed * gain_a[...]
         d_hidden = after[here, :] + scale * (

time: 149 us -> 145 us (0.973)
  Pallas kernels: 148 us -> 144 us
    pallas_call x1, Pallas kernels: 145 us -> 141 us  [local_pass(): pl.pallas_call(kernel, out_shape=[jax.ShapeDtypeStruct((chunks, rows, wid...]
where the time goes in v5:
time: 145 us; the launch traced here: 144 us
  Pallas kernels  144 us (99%)
    pallas_call x1, Pallas kernels, local_pass(): pl.pallas_call(kernel, out_shape=[jax.ShapeDtypeStruct((chunks, rows, wid...  141 us

profile of v5, /device:TPU:0, one launch (start us, length us, event | category | flops | bytes accessed | tf_op | source)
XLA Modules:
  0.0 144.4 jit_solution(3170016557071292647)
XLA Ops:
  0.6 140.9 %shard_map.195 = (bf16[2,256,768]{2,1,0:T(8,128)(2,1)}, bf16[2,256,768]{2,1,0:T(8,128)(2,1)}, f32[2,24,1536]{2,1,0:T(8,128)}, f32[2,24,1536]{2,1,0:T(8,128)}, f3...) custom-call(bf16[2,256,768]{2,1,0:T(8,128)(2,1)} %bitcast.28, ...), custom_call_target="tpu_custom_call" | custom-call | flops 17999998976 | bytes 30000000 | tf_op jit(solution)/shard_map/pallas_call | solution.py:854
  141.5 2.7 %shard_map.196 = (bf16[2,256,768]{2,1,0:T(8,128)(2,1)}, bf16[2,256,768]{2,1,0:T(8,128)(2,1)}, f32[2,24,1536]{2,1,0:T(8,128)}, f32[2,24,1536]{2,1,0:T(8,128)}, f3...) custom-call(bf16[2,256,768]{2,1,0:T(8,128)(2,1)} %get-tuple-element., ...), custom_call_target="tpu_custom_call" | custom-call | tf_op jit(solution)/shard_map/pallas_call | solution.py:889

commit v6 on v5

--- a/solution.py
+++ b/solution.py
@@ -451,19 +451,21 @@
         base = 4 * phase
         own[phase + 1] = (own[phase] + lots[base + 2]) + (lots[base] + lots[base + 1])
 
-    def out_gradients():
+    def expert_gradients(stage, tile, lefts, rights):
         done = 0
-        for piece in pieces[0]:
-            if piece.tile + piece.count > done:
-                until = piece.tile + piece.count
+        for piece in pieces[stage]:
+            until = piece.tile + piece.count - tile
+            if until > done:
                 until += until % 4
-                product_tiles(done, rt, act2, until - done, done)
+                product_tiles(tile + done, lefts, rights, until - done, done)
                 done = until
             piece.open()
 
+    def out_gradients():
+        expert_gradients(0, 0, rt, act2)
+
     def in_gradients():
-        product_tiles(out_tiles, nt, back2, out_tiles)
-        begin(1)
+        expert_gradients(1, out_tiles, nt, back2)
         relay(0, 0, False)
 
     @pl.when(first)

time: 145 us -> 145 us (level)
  no operation moved by 1% of the time
where the time goes in v6:
time: 145 us; the launch traced here: 144 us
  Pallas kernels  144 us (99%)
    pallas_call x1, Pallas kernels, local_pass(): pl.pallas_call(kernel, out_shape=[jax.ShapeDtypeStruct((chunks, rows, wid...  141 us

profile of v6, /device:TPU:0, one launch (start us, length us, event | category | flops | bytes accessed | tf_op | source)
XLA Modules:
  0.0 144.4 jit_solution(11444195042058854530)
XLA Ops:
  0.6 140.9 %shard_map.195 = (bf16[2,256,768]{2,1,0:T(8,128)(2,1)}, bf16[2,256,768]{2,1,0:T(8,128)(2,1)}, f32[2,24,1536]{2,1,0:T(8,128)}, f32[2,24,1536]{2,1,0:T(8,128)}, f3...) custom-call(bf16[2,256,768]{2,1,0:T(8,128)(2,1)} %bitcast.28, ...), custom_call_target="tpu_custom_call" | custom-call | flops 17999998976 | bytes 30000000 | tf_op jit(solution)/shard_map/pallas_call | solution.py:856
  141.5 2.7 %shard_map.196 = (bf16[2,256,768]{2,1,0:T(8,128)(2,1)}, bf16[2,256,768]{2,1,0:T(8,128)(2,1)}, f32[2,24,1536]{2,1,0:T(8,128)}, f32[2,24,1536]{2,1,0:T(8,128)}, f3...) custom-call(bf16[2,256,768]{2,1,0:T(8,128)(2,1)} %get-tuple-element., ...), custom_call_target="tpu_custom_call" | custom-call | tf_op jit(solution)/shard_map/pallas_call | solution.py:891
